TPU v7x, 32 devices: a whole 2x2x4 slice. The times are simulated.
32 devices in a mesh: section: 4 (over y, x), batch: 8 (over z, core).
Axes of the slice: x: 2, y: 2, z: 4, core: 2. Of those that a mesh axis runs over, the one named last changes fastest.
Arguments:
- tokens: bfloat16 [4096, 1024], P('batch'), may hold values from -6 to 6
- cotangent: bfloat16 [4096, 1024], P('batch'), may hold values from -6 to 6
- params: bfloat16 [4, 8455168], P('section'), may hold values from -4 to 4
- lengths: int32 [8, 2, 4], P('batch'), may hold values from 1 to 160, 256 in all within a row
Outputs:
- activations: bfloat16 [4, 4096, 1024], P('section', 'batch')
- input_grads: float32 [4, 4096, 1024], P('section', 'batch')
- weight_grads: float32 [4, 8455168], P('section', 'batch')
Inputs may be any that keep to these rules, and one draw needn't show every extreme that they name: Each row of lengths sums to 256, and its largest entry is exactly 160.
All inputs are finite; a program needn't handle non-finite values.
Results may differ from a plain program's by a relative error of at most 0.02.
Values may be sent and summed in bfloat16 or wider, within the bound.
A program may use at most 448 MiB of HBM per device.

v0:
```python
import functools
import math

import jax
import jax.numpy as jnp
from jax import lax
from jax.experimental import pallas as pl
from jax.experimental.pallas import tpu as pltpu
from jax.sharding import PartitionSpec as P

D = 1024
FF = 2752
FP = 2816
HEADS = 16
FEAT = 16
WIN = 64
MICRO = 2
LEN = 256
EPSILON = 1e-06
SCALE = 1.0 / math.sqrt(D)
LINEAR, FEED, WINDOW, FEED2 = 0, 1, 2, 3
MIB = 2**20
MESH = pl.DeviceIdType.MESH
BF = jnp.bfloat16
F32 = jnp.float32


def any_spec():
    return pl.BlockSpec(memory_space=pl.ANY)


def vmem_spec():
    return pl.BlockSpec(memory_space=pltpu.VMEM)


def dot(left, right):
    return jnp.dot(left, right, preferred_element_type=F32)


def dot_t(left, right):
    return lax.dot_general(left, right, (((1,), (1,)), ((), ())), preferred_element_type=F32)


def dot_0(left, right):
    return lax.dot_general(left, right, (((0,), (0,)), ((), ())), preferred_element_type=F32)


def is_feed(section):
    return (section == FEED) | (section == FEED2)


PAIR_STEP = 32 * FF
ROW_STEP = 64 * D
AHEAD = 8


def prepare(section, flat, wide_v, tall_v, chunk, blocks, woven, load_sem):
    def run(steps, count, first, work):
        def load(i):
            slot = lax.rem(i, AHEAD)
            return pltpu.make_async_copy(
                flat.at[:, pl.ds(pl.multiple_of(first + i * count, 1024), count)],
                chunk.at[slot, :, pl.ds(0, count)],
                load_sem.at[slot],
            )

        def start(i, carry):
            load(i).start()
            return carry

        lax.fori_loop(0, AHEAD, start, 0)

        def step(i, carry):
            load(i).wait()
            rows = count // 128
            blocks[pl.ds(0, rows), :] = chunk[lax.rem(i, AHEAD), :, pl.ds(0, count)].astype(F32).reshape(rows, 128)
            work(i)

            @pl.when(i + AHEAD < steps)
            def _():
                load(i + AHEAD).start()

            return carry

        lax.fori_loop(0, steps, step, 0)

    def rows_of(index, count):
        return pl.ds(pl.multiple_of(index * count, count), count)

    def pair_work(i):
        low_half = lax.broadcasted_iota(jnp.int32, (16, 128), 1) < 64
        rolled = pltpu.roll(blocks[pl.ds(21, 16, stride=43), :], 64, 1)
        for c in range(22):
            even = blocks[pl.ds(c, 16, stride=43), :]
            if c == 21:
                even = jnp.where(low_half, even, 0.0)
                odd = jnp.where(low_half, rolled, 0.0)
            else:
                after = pltpu.roll(blocks[pl.ds(22 + c, 16, stride=43), :], 64, 1)
                odd = jnp.where(low_half, rolled, after)
                rolled = after
            woven[c, pl.ds(0, 16, stride=2), :] = even
            woven[c, pl.ds(1, 16, stride=2), :] = odd
        rows = rows_of(lax.rem(i, 32), 32)
        for c in range(22):
            wide_v[i // 32, rows, pl.ds(128 * c, 128)] = woven[c].astype(BF)

    def row_work(target, rows, first_col):
        for c in range(8):
            target[rows, pl.ds(first_col + 128 * c, 128)] = blocks[pl.ds(c, 64, stride=8), :].astype(BF)

    def square(i, first, target, first_col):
        @pl.when((i >= first) & (i < first + 16))
        def _():
            row_work(target, rows_of(i - first, 64), first_col)

    @pl.when(is_feed(section))
    def _():
        run(64, PAIR_STEP, D, pair_work)
        run(43, ROW_STEP, D + 2 * D * FF, lambda i: row_work(tall_v, rows_of(i, 64), 0))
        tall_v[pl.ds(FF, FP - FF), :] = jnp.zeros((FP - FF, D), BF)

    @pl.when(section == WINDOW)
    def _():
        def work(i):
            square(i, 0, wide_v.at[0], 0)
            square(i, 16, wide_v.at[0], D)
            square(i, 32, wide_v.at[1], 0)
            square(i, 48, tall_v, 0)

        run(64, ROW_STEP, D, work)

    @pl.when(section == LINEAR)
    def _():
        def work(i):
            for part in range(2):

                @pl.when(i // 4 == part)
                def _(part=part):
                    rows = rows_of(i - 4 * part, 256)
                    for c in range(2):
                        cols = pl.ds(part * HEADS * FEAT + 128 * c, 128)
                        wide_v[0, rows, cols] = blocks[pl.ds(c, 256, stride=2), :].astype(BF)

            square(i, 8, wide_v.at[1], 0)
            square(i, 24, tall_v, 0)

        run(40, ROW_STEP, D, work)


ROWS = 128
CHUNKS_OF = LEN // ROWS


def lanes_of_head(kind, block, half):
    lanes = lax.broadcasted_iota(jnp.int32, (1, 128), 1)
    if kind == WINDOW:
        return lanes // 64 == half
    return lanes // FEAT == lax.rem(2 * block + half, 8)


def lanes_of_value(half):
    return lax.broadcasted_iota(jnp.int32, (1, 128), 1) // 64 == half


def only(mask, values):
    return jnp.where(mask, values, jnp.zeros_like(values))


def both(masks, values):
    return jnp.concatenate([only(masks[0], values), only(masks[1], values)], axis=0)


def merge(masks, stacked):
    return only(masks[0], stacked[:ROWS]) + only(masks[1], stacked[ROWS:])


def block_of(index, first=0):
    return pl.ds(pl.multiple_of(first + index * 128, 128), 128)


def query_index(kind, block):
    return block if kind == WINDOW else block // 4


def low_width(kind):
    return D if kind == WINDOW else HEADS * FEAT


def mask_of(kind, doc_col, doc_row, first_row):
    shape = (doc_col.shape[0], doc_row.shape[1])
    rows = lax.broadcasted_iota(jnp.int32, shape, 0) + first_row
    cols = lax.broadcasted_iota(jnp.int32, shape, 1)
    mask = (doc_col == doc_row) & (cols <= rows)
    if kind == WINDOW:
        mask = mask & (rows - cols < WIN)
    return mask.astype(F32)


def root_of(kind):
    return 1.0 / math.sqrt(D // HEADS if kind == WINDOW else FEAT)


def out_scale(kind):
    return {LINEAR: 8.0, WINDOW: 4.0, FEED: 1.0}[kind] * SCALE


def train_kernel(
    swapping,
    tokens, cotangent, flat, docs,
    acts, d_inputs, normed, middle, d_first, d_second, grads, d_gain,
    wide_v, tall_v, gain_v, docs_v, z_v, h_v, x_v, g_v, dz_v, first_v, second_v, mid_v, dh_v, gain_sum, far_gain,
    raised_v, slope_v, inverse_v, mask_v, dy_v, dq_v, dk_v, dv_v, chunk, blocks, woven,
    load_sem, gain_sem, in_sem, act_sem, out_sem, on_send, on_recv, back_send, back_recv, far_send, far_recv,
):
    section = lax.axis_index("section")
    batch = lax.axis_index("batch")
    last = lax.axis_size("section") - 1
    batches = lax.axis_size("batch")
    steps = MICRO * CHUNKS_OF
    count = steps * ROWS
    barrier = pltpu.get_barrier_semaphore()

    far = lax.rem(batch + batches // 2, batches)
    nobody = section < 0
    lower = batch < batches // 2
    gives = is_feed(section) | ((section == WINDOW) & jnp.logical_not(lower)) if swapping else nobody
    takes = is_feed(section) | ((section == WINDOW) & lower) if swapping else nobody

    @pl.when(gives | takes)
    def _():
        pl.semaphore_signal(barrier, inc=1, device_id=(section, far), device_id_type=MESH)

    @pl.when(section > 0)
    def _():
        pl.semaphore_signal(barrier, inc=1, device_id=(section - 1, batch), device_id_type=MESH)

    @pl.when(section < last)
    def _():
        pl.semaphore_signal(barrier, inc=1, device_id=(section + 1, batch), device_id_type=MESH)

    gain_copy = pltpu.make_async_copy(flat.at[:, pl.ds(0, D)], gain_v, gain_sem)
    gain_copy.start()
    token_copy = pltpu.make_async_copy(tokens, z_v.at[pl.ds(0, count), :], in_sem.at[0])
    tangent_copy = pltpu.make_async_copy(cotangent, g_v.at[pl.ds(0, count), :], in_sem.at[1])

    @pl.when(section == 0)
    def _():
        token_copy.start()

    @pl.when(section == last)
    def _():
        tangent_copy.start()

    docs_v[pl.ds(0, MICRO)] = docs[...]
    prepare(section, flat, wide_v, tall_v, chunk, blocks, woven, load_sem)
    gain_copy.wait()
    gain = 1.0 + gain_v[...].astype(F32) / 8.0
    gain_sum[...] = jnp.zeros_like(gain_sum)

    @pl.when(section == 0)
    def _():
        token_copy.wait()

    @pl.when(section == last)
    def _():
        tangent_copy.wait()

    greeted = jnp.where((section > 0) & (section < last), 2, 1)
    pl.semaphore_wait(barrier, greeted + jnp.where(gives | takes, 1, 0))

    def rows_at(step, phase=0):
        return pl.ds(pl.multiple_of(phase * count + step * ROWS, ROWS), ROWS)

    def hand_on(step):
        rows = rows_at(step)
        return pltpu.make_async_remote_copy(
            src_ref=x_v.at[rows, :],
            dst_ref=z_v.at[rows, :],
            send_sem=on_send.at[step],
            recv_sem=on_recv.at[step],
            device_id=(section + 1, batch),
            device_id_type=MESH,
        )

    def hand_back(step):
        rows = rows_at(step)
        return pltpu.make_async_remote_copy(
            src_ref=x_v.at[rows, :],
            dst_ref=g_v.at[rows, :],
            send_sem=back_send.at[step],
            recv_sem=back_recv.at[step],
            device_id=(section - 1, batch),
            device_id_type=MESH,
        )

    def far_copy(kind, step=0):
        rows, target = rows_at(step), rows_at(step, 1)
        source, target = (
            (z_v.at[rows, :], z_v.at[target, :]),
            (g_v.at[rows, :], g_v.at[target, :]),
            (gain_sum, far_gain),
            (docs_v.at[pl.ds(0, MICRO)], docs_v.at[pl.ds(MICRO, MICRO)]),
        )[kind]
        return pltpu.make_async_remote_copy(
            src_ref=source,
            dst_ref=target,
            send_sem=far_send.at[kind, step],
            recv_sem=far_recv.at[kind, step],
            device_id=(section, far),
            device_id_type=MESH,
        )

    @pl.when(gives)
    def _():
        far_copy(3).start()

    @pl.when(gives & (section == last))
    def _():
        for step in range(steps):
            far_copy(1, step).start()

    def act_out(step):
        rows = rows_at(step)
        return pltpu.make_async_copy(x_v.at[rows, :], acts.at[rows, :], act_sem.at[0, step])

    def forward_outs(phase, step):
        rows, target = rows_at(step), rows_at(step, phase)
        return [
            pltpu.make_async_copy(h_v.at[rows, :], normed.at[target, :], act_sem.at[1, step]),
            pltpu.make_async_copy(mid_v.at[rows, :], middle.at[target, :], act_sem.at[2, step]),
        ]

    def gradient_out(step):
        rows = rows_at(step)
        return pltpu.make_async_copy(dz_v.at[rows, :], d_inputs.at[rows, :], out_sem.at[0, step])

    def backward_outs(phase, step):
        rows, target = rows_at(step), rows_at(step, phase)
        return [
            pltpu.make_async_copy(g_v.at[target, :], grads.at[target, :], out_sem.at[1, step]),
            pltpu.make_async_copy(first_v.at[rows, :], d_first.at[target, :], out_sem.at[2, step]),
            pltpu.make_async_copy(second_v.at[rows, :], d_second.at[target, :], out_sem.at[3, step]),
        ]


    def forward_step(phase, step, hidden, project):
        rows, here = rows_at(step), rows_at(step, phase)
        own = phase == 0

        @pl.when(own & (section > 0))
        def _():
            hand_on(step).wait_recv()

        @pl.when(own & gives)
        def _():
            far_copy(0, step).start()

        @pl.when(jnp.logical_not(own))
        def _():
            far_copy(0, step).wait_recv()

        z = z_v[here, :].astype(F32)
        scaled = lax.rsqrt(jnp.mean(z * z, axis=1, keepdims=True) + EPSILON)
        h_v[rows, :] = (z * scaled * gain).astype(BF)
        hidden(rows)

        @pl.when(own)
        def _():
            x_v[rows, :] = (z_v[here, :].astype(F32) + project(rows)).astype(BF)

            @pl.when(section < last)
            def _():
                hand_on(step).start()

            act_out(step).start()

        for copy in forward_outs(phase, step):
            copy.start()

    def backward_step(phase, step, unhidden, back):
        rows, here = rows_at(step), rows_at(step, phase)
        own = phase == 0

        @pl.when(own & (section < last))
        def _():
            hand_back(step).wait_recv()

            @pl.when(gives)
            def _():
                far_copy(1, step).start()

        @pl.when(jnp.logical_not(own))
        def _():
            far_copy(1, step).wait_recv()

        unhidden(here, rows)

        @pl.when(own)
        def _():
            dh_v[...] = back(rows) * SCALE
            z = z_v[rows, :].astype(F32)
            scaled = lax.rsqrt(jnp.mean(z * z, axis=1, keepdims=True) + EPSILON)
            unit = z * scaled
            d_normed = dh_v[...]
            gain_sum[0:1, :] += jnp.sum(d_normed * unit, axis=0, keepdims=True) * 0.125
            d_unit = d_normed * gain
            d_z = scaled * (d_unit - unit * jnp.mean(d_unit * unit, axis=1, keepdims=True))
            d_z += g_v[rows, :].astype(F32)
            dz_v[rows, :] = d_z
            x_v[rows, :] = d_z.astype(BF)

            @pl.when(section > 0)
            def _():
                hand_back(step).start()

            gradient_out(step).start()

        for copy in backward_outs(phase, step):
            copy.start()

    def feed_hidden(rows):
        half = FP // 2

        def piece(part, carry):
            cols = pl.ds(pl.multiple_of(part * half, half), half)
            gate = dot(h_v[rows, :], wide_v[0, :, cols]) * SCALE
            up = dot(h_v[rows, :], wide_v[1, :, cols]) * SCALE
            sig = 1.0 / (1.0 + jnp.exp(-gate))
            silu = gate * sig
            first_v[rows, cols] = (up * (sig + silu * (1.0 - sig))).astype(BF)
            second_v[rows, cols] = silu.astype(BF)
            mid_v[rows, cols] = (silu * up).astype(BF)
            return carry

        lax.fori_loop(0, 2, piece, 0)

    def feed_project(rows):
        return dot(mid_v[rows, :], tall_v[...]) * SCALE

    def feed_unhidden(here, rows):
        half = FP // 2

        def piece(part, carry):
            cols = pl.ds(pl.multiple_of(part * half, half), half)
            d_mid = dot_t(g_v[here, :], tall_v[cols, :]) * SCALE
            first_v[rows, cols] = (d_mid * first_v[rows, cols].astype(F32)).astype(BF)
            second_v[rows, cols] = (d_mid * second_v[rows, cols].astype(F32)).astype(BF)
            return carry

        lax.fori_loop(0, 2, piece, 0)

    def feed_back(rows):
        return dot_t(first_v[rows, :], wide_v[0]) + dot_t(second_v[rows, :], wide_v[1])

    def attend_hidden(kind, phase, micro, part, rows):
        width = low_width(kind)
        span = ROWS * (part + 1)
        keys_at = pl.ds(pl.multiple_of(micro * LEN, LEN), span)
        step = micro * CHUNKS_OF + part
        first_v[rows, pl.ds(0, 2 * width)] = (dot(h_v[rows, :], wide_v[0, :, pl.ds(0, 2 * width)]) * SCALE).astype(BF)
        second_v[rows, pl.ds(0, D)] = (dot(h_v[rows, :], wide_v[1, :, pl.ds(0, D)]) * SCALE).astype(BF)
        cols = pl.ds(0, span)
        index = phase * MICRO + micro
        own_docs = jnp.broadcast_to(docs_v[index, :, pl.ds(part * ROWS, ROWS)], (8, ROWS))
        mask_v[:, cols] = mask_of(kind, own_docs.T[:, 0:1], docs_v[index, :, cols], part * ROWS)

        def block(t, carry):
            index = query_index(kind, t)
            queries = first_v[rows, block_of(index)]
            keys = first_v[keys_at, block_of(index, width)]
            values = second_v[keys_at, block_of(t)]
            heads = [lanes_of_head(kind, t, half) for half in range(2)]
            scores = (dot_t(both(heads, queries), keys) * root_of(kind)).reshape(2, ROWS, span)
            mask = mask_v[:, cols]
            if kind == WINDOW:
                kept = jnp.where((mask > 0.0)[None], scores, -1e30)
                raised = jnp.exp(kept - jnp.max(kept, axis=2, keepdims=True))
            else:
                slope = mask[None] * (1.0 + scores)
                slope_v[step, t, :, cols] = slope.astype(BF).reshape(2 * ROWS, span)
                raised = 0.5 * (mask[None] + slope * slope)
            raised = raised.astype(BF).reshape(2 * ROWS, span)
            raised_v[step, t, :, cols] = raised
            summed = dot(raised, jnp.concatenate([values, jnp.ones((span, 128), BF)], axis=1))
            inverse = 1.0 / summed[:, 128:]
            sides = [lanes_of_value(half) for half in range(2)]
            mid_v[rows, block_of(t)] = merge(sides, summed[:, :128] * inverse).astype(BF)
            inverse_v[rows, block_of(t)] = merge(sides, inverse)
            return carry

        lax.fori_loop(0, 8, block, 0, unroll=UNROLL)

    def attend_project(kind, rows):
        return dot(mid_v[rows, pl.ds(0, D)], tall_v[pl.ds(0, D), :]) * out_scale(kind)

    def attend_unhidden(kind, micro, part, here, rows):
        width = low_width(kind)
        span = ROWS * (part + 1)
        keys_at = pl.ds(pl.multiple_of(micro * LEN, LEN), span)
        own = pl.ds(0, span)
        step = micro * CHUNKS_OF + part
        d_mixed = dot_t(g_v[here, :], tall_v[pl.ds(0, D), :]) * out_scale(kind)
        dy_v[...] = (d_mixed * inverse_v[rows, :]).astype(BF)
        if part == CHUNKS_OF - 1:
            dk_v[...] = jnp.zeros_like(dk_v)
            dv_v[...] = jnp.zeros_like(dv_v)
        if kind == LINEAR:
            dq_v[...] = jnp.zeros_like(dq_v)

        def block(t, carry):
            index = query_index(kind, t)
            queries = first_v[rows, block_of(index)]
            keys = first_v[keys_at, block_of(index, width)]
            values = second_v[keys_at, block_of(t)]
            heads = [lanes_of_head(kind, t, half) for half in range(2)]
            sides = [lanes_of_value(half) for half in range(2)]
            d_mixed = both(sides, dy_v[:, block_of(t)])
            mixed = mid_v[rows, block_of(t)].astype(F32)
            shift = jnp.sum(d_mixed.astype(F32) * jnp.concatenate([mixed, mixed], axis=0), axis=1, keepdims=True)
            d_weights = dot_t(d_mixed, values) - shift
            raised = raised_v[step, t, :, own]
            slope = raised if kind == WINDOW else slope_v[step, t, :, own]
            d_scores = (slope.astype(F32) * d_weights).astype(BF)
            dv_v[own, block_of(t)] += dot_0(raised, d_mixed)
            d_queries = merge(heads, dot(d_scores, keys)) * root_of(kind)
            dk_v[own, block_of(index)] += dot_0(d_scores, both(heads, queries)) * root_of(kind)
            if kind == WINDOW:
                dq_v[:, block_of(t)] = d_queries
            else:
                dq_v[:, block_of(index)] += d_queries
            return carry

        lax.fori_loop(0, 8, block, 0, unroll=UNROLL)
        done = pl.ds(part * ROWS, ROWS)
        first_v[rows, pl.ds(0, width)] = dq_v[:, pl.ds(0, width)].astype(BF)
        first_v[rows, pl.ds(width, width)] = dk_v[done, pl.ds(0, width)].astype(BF)
        second_v[rows, pl.ds(0, D)] = dv_v[done, :].astype(BF)

    def attend_back(kind, rows):
        width = low_width(kind)
        total = dot_t(first_v[rows, pl.ds(0, 2 * width)], wide_v[0, :, pl.ds(0, 2 * width)])
        total += dot_t(second_v[rows, pl.ds(0, D)], wide_v[1, :, pl.ds(0, D)])
        return total

    def one_phase(phase, carry):
        own = phase == 0

        @pl.when(is_feed(section))
        def _():
            def forward(step, inner):
                forward_step(phase, step, feed_hidden, feed_project)
                return inner

            lax.fori_loop(0, steps, forward, 0)

        for kind in (WINDOW, LINEAR):

            @pl.when(section == kind)
            def _(kind=kind):
                def forward(micro, inner):
                    for part in range(CHUNKS_OF):
                        forward_step(
                            phase,
                            micro * CHUNKS_OF + part,
                            functools.partial(attend_hidden, kind, phase, micro, part),
                            functools.partial(attend_project, kind),
                        )
                    return inner

                lax.fori_loop(0, MICRO, forward, 0)

        def settle(step, inner):
            @pl.when(own)
            def _():
                @pl.when(section < last)
                def _():
                    hand_on(step).wait_send()

                act_out(step).wait()

            for copy in forward_outs(phase, step):
                copy.wait()
            return inner

        lax.fori_loop(0, steps, settle, 0)

        @pl.when(is_feed(section))
        def _():
            def backward(step, inner):
                micro, part = step // CHUNKS_OF, CHUNKS_OF - 1 - lax.rem(step, CHUNKS_OF)
                backward_step(phase, micro * CHUNKS_OF + part, feed_unhidden, feed_back)
                return inner

            lax.fori_loop(0, steps, backward, 0)

        for kind in (WINDOW, LINEAR):

            @pl.when(section == kind)
            def _(kind=kind):
                def backward(micro, inner):
                    for part in reversed(range(CHUNKS_OF)):
                        backward_step(
                            phase,
                            micro * CHUNKS_OF + part,
                            functools.partial(attend_unhidden, kind, micro, part),
                            functools.partial(attend_back, kind),
                        )
                    return inner

                lax.fori_loop(0, MICRO, backward, 0)

        @pl.when(own & gives)
        def _():
            far_copy(2).start()

        def finish(step, inner):
            @pl.when(own)
            def _():
                @pl.when(section > 0)
                def _():
                    hand_back(step).wait_send()

                gradient_out(step).wait()

            for copy in backward_outs(phase, step):
                copy.wait()
            return inner

        lax.fori_loop(0, steps, finish, 0)

        @pl.when(own & takes)
        def _():
            far_copy(3).wait_recv()

        return carry

    lax.fori_loop(0, jnp.where(takes, 2, 1), one_phase, 0)
    d_gain[...] = gain_sum[...]

    @pl.when(takes)
    def _():
        far_copy(2).wait_recv()
        d_gain[...] += far_gain[...]

    @pl.when(gives)
    def _():
        for kind in range(2):
            for step in range(steps):
                far_copy(kind, step).wait_send()
        far_copy(2).wait_send()
        far_copy(3).wait_send()


UNROLL = 2


def train(tokens, cotangent, flat, docs, swapping):
    count = MICRO * LEN
    steps = MICRO * CHUNKS_OF
    kept = 2 * count if swapping else count
    return pl.pallas_call(
        functools.partial(train_kernel, swapping),
        out_shape=(
            jax.ShapeDtypeStruct((count, D), BF),
            jax.ShapeDtypeStruct((count, D), F32),
            jax.ShapeDtypeStruct((kept, D), BF),
            jax.ShapeDtypeStruct((kept, FP), BF),
            jax.ShapeDtypeStruct((kept, FP), BF),
            jax.ShapeDtypeStruct((kept, FP), BF),
            jax.ShapeDtypeStruct((kept, D), BF),
            jax.ShapeDtypeStruct((8, D), F32),
        ),
        in_specs=[any_spec()] * 3 + [vmem_spec()],
        out_specs=(any_spec(),) * 7 + (vmem_spec(),),
        scratch_shapes=[
            pltpu.VMEM((2, D, FP), BF),
            pltpu.VMEM((FP, D), BF),
            pltpu.VMEM((1, D), BF),
            pltpu.VMEM((2 * MICRO, 1, LEN), F32),
            pltpu.VMEM((2 * count, D), BF),
            pltpu.VMEM((count, D), BF),
            pltpu.VMEM((count, D), BF),
            pltpu.VMEM((2 * count, D), BF),
            pltpu.VMEM((count, D), F32),
            pltpu.VMEM((count, FP), BF),
            pltpu.VMEM((count, FP), BF),
            pltpu.VMEM((count, FP), BF),
            pltpu.VMEM((ROWS, D), F32),
            pltpu.VMEM((8, D), F32),
            pltpu.VMEM((8, D), F32),
            pltpu.VMEM((steps, 8, 2 * ROWS, LEN), BF),
            pltpu.VMEM((steps, 8, 2 * ROWS, LEN), BF),
            pltpu.VMEM((count, D), F32),
            pltpu.VMEM((ROWS, LEN), F32),
            pltpu.VMEM((ROWS, D), BF),
            pltpu.VMEM((ROWS, D), F32),
            pltpu.VMEM((LEN, D), F32),
            pltpu.VMEM((LEN, D), F32),
            pltpu.VMEM((AHEAD, 1, PAIR_STEP), BF),
            pltpu.VMEM((PAIR_STEP // 128, 128), F32),
            pltpu.VMEM((22, 32, 128), F32),
            pltpu.SemaphoreType.DMA((AHEAD,)),
            pltpu.SemaphoreType.DMA,
            pltpu.SemaphoreType.DMA((2,)),
            pltpu.SemaphoreType.DMA((3, steps)),
            pltpu.SemaphoreType.DMA((4, steps)),
            pltpu.SemaphoreType.DMA((steps,)),
            pltpu.SemaphoreType.DMA((steps,)),
            pltpu.SemaphoreType.DMA((steps,)),
            pltpu.SemaphoreType.DMA((steps,)),
            pltpu.SemaphoreType.DMA((4, steps)),
            pltpu.SemaphoreType.DMA((4, steps)),
        ],
        compiler_params=pltpu.CompilerParams(
            collective_id=0, has_side_effects=True, vmem_limit_bytes=62 * MIB
        ),
        name="train",
    )(tokens, cotangent, flat, docs)


HEAD_ROWS = 16
PAIR_ROWS = 128 * 43
CHUNKS = 11


class Products:
    def __init__(self, sources, scratch, base):
        self.normed, self.d_first, self.d_second, self.middle, self.grads, self.d_gain = sources
        self.left_v, self.d_v, self.woven, self.stage, self.in_sem = scratch
        self.base = base

    def fetch(self, source, target, index):
        return pltpu.make_async_copy(source, target, self.in_sem.at[index])

    def loads(self, names):
        count = self.left_v.shape[1]
        some = pl.ds(0, MICRO * LEN)
        every = pl.ds(0, count)
        low, both, high = pl.ds(0, D), pl.ds(0, 2 * D), pl.ds(D, D)
        table = {
            "h": (self.normed, self.left_v.at[0], 0),
            "g": (self.grads, self.left_v.at[1], 1),
            "first": (self.d_first, self.d_v.at[0], 2),
            "second": (self.d_second, self.d_v.at[1], 3),
            "middle": (self.middle, self.d_v.at[self.middle_slot()], 4),
        }
        for prefix, rows in (("all_", every), ("some_", some)):
            table[prefix + "h"] = (self.normed.at[rows, :], self.left_v.at[0, rows, :], 0)
            table[prefix + "mixed"] = (self.middle.at[rows, low], self.left_v.at[1, rows, :], 1)
            table[prefix + "low"] = (self.d_first.at[rows, both], self.d_v.at[0, rows, both], 2)
            table[prefix + "value"] = (self.d_second.at[rows, low], self.d_v.at[1, rows, low], 3)
            table[prefix + "g"] = (self.grads.at[rows, :], self.d_v.at[1, rows, high], 4)
        return [self.fetch(*table[name]) for name in names]

    def middle_slot(self):
        return 2 if self.d_v.shape[0] == 3 else 0

    def head(self, out):
        stage = self.stage
        stage[pl.ds(0, 8), :] = jnp.zeros((8, 128), F32)
        stage[pl.ds(8, 8), :] = self.d_gain[0:1, :].reshape(8, 128)
        out[pl.ds(0, 16), :] = stage[pl.ds(0, 16), :].astype(BF)

    def cut(self, out, first_row, rows, piece, scale):
        target_row = first_row - self.base

        def step(j, carry):
            source = pl.ds(pl.multiple_of(j * piece, 16), piece)
            target = pl.ds(pl.multiple_of(target_row + j * piece, 16), piece)
            out[target, :] = (self.stage[source, :] * scale).astype(BF)
            return carry

        lax.fori_loop(0, rows // piece, step, 0)

    def pairs(self, which, first_pair):
        count = 128
        stage, woven = self.stage, self.woven
        half = FP // 2
        low_half = lax.broadcasted_iota(jnp.int32, (count, 128), 1) < 64
        left = self.left_v[0, :, pl.ds(pl.multiple_of(2 * first_pair, 128), 2 * count)]
        for part in range(2):
            piece = dot_0(left, self.d_v[which, :, pl.ds(part * half, half)])
            for c in range(11):
                woven[11 * part + c, pl.ds(0, 2 * count), :] = piece[:, 128 * c : 128 * c + 128]
        for c in range(22):
            stage[pl.ds(c, count, stride=43), :] = woven[c, pl.ds(0, count, stride=2), :]
        before = woven[21, pl.ds(0, count, stride=2), :]
        for c in range(22):
            here = pltpu.roll(woven[c, pl.ds(1, count, stride=2), :], 64, 1)
            stage[pl.ds(21 + c, count, stride=43), :] = jnp.where(low_half, before, here)
            before = here

    def pair_tile(self, out, k, tail_only):
        self.pairs(k // 4, lax.rem(k, 4) * 128)

        @pl.when(jnp.logical_not(tail_only))
        def _():
            self.cut(out, HEAD_ROWS + k * PAIR_ROWS, PAIR_ROWS, 688, SCALE)

        @pl.when(tail_only)
        def _():
            target = pl.ds(pl.multiple_of((k + 1) * PAIR_ROWS - self.base, 16), 16)
            out[target, :] = (self.stage[pl.ds(PAIR_ROWS - 16, 16), :] * SCALE).astype(BF)

    def tall(self, out, left, right, stride, rows, first_row, scale, piece):
        product = dot_0(left, right)
        for c in range(stride):
            self.stage[pl.ds(c, rows, stride=stride), :] = product[:, 128 * c : 128 * c + 128]
        self.cut(out, first_row, rows * stride, piece, scale)

    def down_tile(self, out, j):
        left = self.d_v[self.middle_slot(), :, pl.ds(pl.multiple_of(256 * j, 256), 256)]
        self.tall(out, left, self.left_v[1], 8, 256, DOWN_ROW + 2048 * j, SCALE, 512)

    def window_tile(self, out, k):
        left = self.left_v[k // 6, :, pl.ds(pl.multiple_of(lax.rem(k, 2) * 512, 512), 512)]
        right = self.d_v[k // 4, :, pl.ds(pl.multiple_of(lax.rem(k // 2, 2) * D, D), D)]
        scale = jnp.where(k < 6, SCALE, out_scale(WINDOW))
        self.tall(out, left, right, 8, 512, HEAD_ROWS + 4096 * k, scale, 512)

    def low_tile(self, out, k):
        some = pl.ds(0, MICRO * LEN)
        width = HEADS * FEAT
        right = self.d_v[0, some, pl.ds(pl.multiple_of(k * width, width), width)]
        self.tall(out, self.left_v[0, some, :], right, 2, D, HEAD_ROWS + k * 2048, SCALE, 512)

    def value_tile(self, out, k):
        some = pl.ds(0, MICRO * LEN)
        left = self.left_v[k // 2, some, pl.ds(pl.multiple_of(lax.rem(k, 2) * 512, 512), 512)]
        right = self.d_v[1, some, pl.ds(pl.multiple_of(k // 2 * D, D), D)]
        scale = jnp.where(k < 2, SCALE, out_scale(LINEAR))
        self.tall(out, left, right, 8, 512, HEAD_ROWS + 4096 * (k + 1), scale, 512)


DOWN_ROW = HEAD_ROWS + 8 * PAIR_ROWS
DOWN_TILES = FP // 256
WINDOW_END = HEAD_ROWS + 4 * 8192
LINEAR_END = HEAD_ROWS + 20480


def each(first, last, act):
    def step(i, carry):
        act(i)
        return carry

    lax.fori_loop(first, last, step, 0)


def product_scratch(count, slots):
    return [
        pltpu.VMEM((2, count, D), BF),
        pltpu.VMEM((slots, count, FP), BF),
        pltpu.VMEM((22, 256, 128), F32),
        pltpu.VMEM((6144, 128), F32),
        pltpu.SemaphoreType.DMA((5,)),
    ]


def clear(out, first_row, rows):
    def step(i, carry):
        out[pl.ds(pl.multiple_of(first_row + i * 128, 16), 128), :] = jnp.zeros((128, 128), BF)
        return carry

    lax.fori_loop(0, rows // 128, step, 0)
    if rows % 128:
        out[pl.ds(first_row + rows // 128 * 128, rows % 128), :] = jnp.zeros((rows % 128, 128), BF)


def products_kernel(*refs):
    section = lax.axis_index("section")
    work = Products(refs[:6], refs[8:], 0)
    out, out_v = refs[6:8]
    total = out_v.shape[0] - 512
    work.head(out_v)

    def load(*names):
        for copy in work.loads(names):
            copy.start()
        for copy in work.loads(names):
            copy.wait()

    @pl.when(is_feed(section))
    def _():
        load("h", "g", "first", "second", "middle")
        each(0, 8, lambda k: work.pair_tile(out_v, k, section < 0))
        each(0, DOWN_TILES, lambda j: work.down_tile(out_v, j))

    for kind in (WINDOW, LINEAR):

        @pl.when(section == kind)
        def _(kind=kind):
            load("some_h", "some_mixed", "some_low", "some_value", "some_g")
            if kind == WINDOW:
                each(0, 8, lambda k: work.window_tile(out_v, k))
            else:
                each(0, 2, lambda k: work.low_tile(out_v, k))
                each(0, 4, lambda k: work.value_tile(out_v, k))
            done = WINDOW_END if kind == WINDOW else LINEAR_END
            clear(out_v, done, total - done)

    store = pltpu.make_async_copy(out_v.at[pl.ds(0, total), :], out, work.in_sem.at[0])
    store.start()
    store.wait()


def products(sources, total_rows):
    return pl.pallas_call(
        products_kernel,
        out_shape=jax.ShapeDtypeStruct((total_rows, 128), BF),
        in_specs=[any_spec()] * 5 + [vmem_spec()],
        out_specs=any_spec(),
        scratch_shapes=[pltpu.VMEM((total_rows + 512, 128), BF)] + product_scratch(MICRO * LEN, 3),
        compiler_params=pltpu.CompilerParams(vmem_limit_bytes=60 * MIB),
        name="products",
    )(*sources)


PLACES = 4


def reduce_kernel(*refs):
    section = lax.axis_index("section")
    batch = lax.axis_index("batch")
    place, core = batch // 2, lax.rem(batch, 2)
    mate = place + 1 - 2 * lax.rem(place, 2)
    out, part, own, passing, total, flat, sems = refs[6:13]
    ex_send, ex_recv, send, recv, out_sem = sems
    width = own.shape[1]
    step_rows = width - HEAD_ROWS
    piece = width // CHUNKS
    feed_here = is_feed(section)
    base = jnp.where(feed_here, place // 2, 0) * (4 * step_rows)
    work = Products(refs[:6], refs[13:], base)
    barrier = pltpu.get_barrier_semaphore()

    def greet(other):
        pl.semaphore_signal(barrier, inc=1, device_id=(section, other), device_id_type=MESH)

    window_here = (section == WINDOW) & (place < 2)
    pair_here = feed_here | window_here
    linear_here = section == LINEAR
    sets = (
        (feed_here & (place < 2), ("h", "first", "second")),
        (feed_here & (place >= 2), ("h", "second", "middle", "g")),
        (window_here, ("all_h", "all_mixed", "all_low", "all_value", "all_g")),
        (linear_here, ("some_h", "some_mixed", "some_low", "some_value", "some_g")),
    )
    for here, names in sets:

        @pl.when(here)
        def _(names=names):
            for copy in work.loads(names):
                copy.start()

    greet(2 * place + 1 - core)

    @pl.when(place > 0)
    def _():
        greet(batch - 2)

    @pl.when(place < PLACES - 1)
    def _():
        greet(batch + 2)

    @pl.when(base == 0)
    def _():
        work.head(part)

    pl.semaphore_wait(barrier, jnp.where((place > 0) & (place < PLACES - 1), 3, 2))
    for here, names in sets:

        @pl.when(here)
        def _(names=names):
            for copy in work.loads(names):
                copy.wait()

    def rows_of(i):
        return pl.ds(pl.multiple_of(i * piece, 16), piece)

    def share(index, i):
        return pl.ds(pl.multiple_of(step_rows * index - base + i * piece, 16), piece)

    def swap(to, i):
        slot = lax.rem(to, 2)
        return pltpu.make_async_remote_copy(
            src_ref=part.at[share(2 * to + 1 - core, i), :],
            dst_ref=own.at[slot, rows_of(i), :],
            send_sem=ex_send.at[slot, i],
            recv_sem=ex_recv.at[slot, i],
            device_id=(section, 2 * place + 1 - core),
            device_id_type=MESH,
        )

    def go(source, slot, to, i, other):
        return pltpu.make_async_remote_copy(
            src_ref=source,
            dst_ref=passing.at[slot, rows_of(i), :],
            send_sem=send.at[lax.rem(to, 2), i],
            recv_sem=recv.at[slot, i],
            device_id=(section, other),
            device_id_type=MESH,
        )

    def arrived(slot, i):
        here = passing.at[slot, rows_of(i), :]
        pltpu.make_async_copy(here, here, recv.at[slot, i]).wait()

    def release(to, before, after, limits=(CHUNKS, CHUNKS)):
        for parity in range(2):

            def bound(row, parity=parity):
                return jnp.minimum(jnp.maximum(row - parity * step_rows, 0) // piece, limits[parity])

            first, last = bound(before), bound(after)

            @pl.when(core != parity)
            def _(first=first, last=last):
                each(first, last, lambda i: swap(to, i).start())

            def add(i):
                slot = lax.rem(to, 2)
                rows = rows_of(i)
                swap(to, i).wait_recv()
                mine = part[share(2 * to + core, i), :].astype(F32)
                own[slot, rows, :] = (own[slot, rows, :].astype(F32) + mine).astype(BF)
                source = own.at[slot, rows, :]

                @pl.when(pair_here & (to == mate))
                def _():
                    go(source, 0, to, i, 2 * mate + core).start()

                @pl.when(linear_here & (place == PLACES - 1))
                def _():
                    go(source, slot, to, i, batch - 2).start()

                @pl.when(linear_here & (place == 0) & (to == 1))
                def _():
                    go(source, 2, to, i, batch + 2).start()

            @pl.when(core == parity)
            def _(first=first, last=last):
                each(first, last, add)

    def swapped(to, limits=(CHUNKS, CHUNKS)):
        each(0, jnp.where(core == 0, limits[1], limits[0]), lambda i: swap(to, i).wait_send())

    def emit(i):
        cols = pl.ds(pl.multiple_of(i * piece * 128, 1024), piece * 128)
        flat[0:1, cols] = total[...].reshape(1, piece * 128)

    whole = 2 * step_rows + HEAD_ROWS

    @pl.when(feed_here)
    def _():
        upper = place >= 2

        def pair(t):
            k = jnp.where(upper, 5 + t, lax.rem(t + jnp.where(place == 0, 2, 0), 6))
            tail_only = upper & (t == 0)
            work.pair_tile(part, k, tail_only)
            start = HEAD_ROWS + PAIR_ROWS * k - base
            stop = start + PAIR_ROWS
            early = jnp.where(k == 1, whole, jnp.where(k < 1, stop, start))
            stop_0 = jnp.where(place == 0, early, stop)
            to = base // (2 * step_rows)
            release(to, jnp.where(tail_only, 0, start), jnp.where(tail_only, 0, stop_0))
            release(to + 1, start - 2 * step_rows, stop - 2 * step_rows)

        def down(j):
            work.down_tile(part, j)
            start = DOWN_ROW + 2048 * j - base
            stop = start + 2048
            early = jnp.where(j == 1, whole, jnp.where(j < 1, stop, start))
            release(2, start, jnp.where(place == 2, early, stop))
            release(3, start - 2 * step_rows, stop - 2 * step_rows)

        def turn(t):
            @pl.when(t == 1)
            def _():
                each(0, jnp.where(upper, 3, 6), pair)

            mate_first = place == 2
            first = jnp.where(mate_first & (t == 0), 2, 0)
            last = jnp.where(mate_first & (t == 1), 2, DOWN_TILES)
            here = upper & (mate_first | (t == 1))
            each(first, jnp.where(here, last, first), down)

        each(0, 2, turn)
        swapped(mate)
        swapped(place)

    @pl.when(window_here)
    def _():
        def tile(t, carry):
            k = lax.rem(t + jnp.where(place == 0, 4, 0), 8)
            work.window_tile(part, k)
            start = HEAD_ROWS + 4096 * k
            stop = start + 4096

            @pl.when(k == 7)
            def _():
                clear(part, WINDOW_END, 4 * step_rows + HEAD_ROWS - WINDOW_END)

            stop_0 = jnp.where(place == 0, jnp.where(k < 3, stop, jnp.where(k == 3, whole, start)), stop)
            stop_1 = jnp.where(k == 7, whole, stop - 2 * step_rows)
            release(0, start, stop_0)
            release(1, start - 2 * step_rows, stop_1)
            return carry

        lax.fori_loop(0, 8, tile, 0)
        for to in range(2):
            swapped(to)

    @pl.when(linear_here)
    def _():
        filled = [max(0, min(CHUNKS, -(-(LINEAR_END - step_rows * index) // piece))) for index in range(4)]
        limits = (tuple(filled[:2]), tuple(filled[2:]))
        cover = max(step_rows * index + piece * filled[index] for index in range(4) if filled[index])
        clear(part, LINEAR_END, cover - LINEAR_END)

        def low(k):
            work.low_tile(part, k)
            start = HEAD_ROWS + 2048 * k
            release(0, start, start + 2048, limits[0])

        def value(k):
            work.value_tile(part, k)
            start = HEAD_ROWS + 4096 * (k + 1)
            stop = jnp.where(k == 3, cover, start + 4096)
            release(0, start, stop, limits[0])
            release(1, start - 2 * step_rows, stop - 2 * step_rows, limits[1])

        each(0, 2, low)
        each(0, 4, value)

        def own_count(to):
            return jnp.where(core == 0, limits[to][0], limits[to][1])

        def pass_down(to):
            def act(i):
                rows = rows_of(i)
                arrived(to, i)
                added = passing[to, rows, :].astype(F32) + own[to, rows, :].astype(F32)
                passing[to, rows, :] = added.astype(BF)
                go(passing.at[to, rows, :], to, to, i, batch - 2).start()

            each(0, own_count(to), act)

        @pl.when((place == 1) | (place == 2))
        def _():
            pass_down(0)

        @pl.when(place == 2)
        def _():
            pass_down(1)

        for to in range(2):
            swapped(to, limits[to])

        def sum_up(i):
            rows = rows_of(i)

            @pl.when((place == 0) & (i < own_count(0)))
            def _():
                arrived(0, i)
                total[...] = own[0, rows, :].astype(F32) + passing[0, rows, :].astype(F32)

            @pl.when((place == 1) & (i < own_count(1)))
            def _():
                arrived(1, i)
                arrived(2, i)
                both_ways = passing[1, rows, :].astype(F32) + passing[2, rows, :].astype(F32)
                total[...] = own[1, rows, :].astype(F32) + both_ways

            here = jnp.where(place == 0, own_count(0), jnp.where(place == 1, own_count(1), 0))

            @pl.when(i >= here)
            def _():
                total[...] = jnp.zeros_like(total)

            emit(i)

        each(0, CHUNKS, sum_up)

        @pl.when((place == 1) | (place >= 2))
        def _():
            each(0, own_count(0), lambda i: go(passing.at[0, rows_of(i), :], 0, 0, i, batch - 2).wait_send())

        @pl.when((place == 0) | (place >= 2))
        def _():
            each(0, own_count(1), lambda i: go(passing.at[0, rows_of(i), :], 0, 1, i, batch - 2).wait_send())

    @pl.when((section == WINDOW) & (place >= 2))
    def _():
        total[...] = jnp.zeros_like(total)
        each(0, CHUNKS, emit)

    @pl.when(pair_here)
    def _():
        slot = lax.rem(place, 2)

        def sum_up(i):
            rows = rows_of(i)
            arrived(0, i)
            total[...] = own[slot, rows, :].astype(F32) + passing[0, rows, :].astype(F32)
            emit(i)

        each(0, CHUNKS, sum_up)
        other = 2 * mate + core
        each(0, CHUNKS, lambda i: go(passing.at[0, rows_of(i), :], 0, mate, i, other).wait_send())

    count = out.shape[1]
    first = pl.multiple_of((8 + batch) * 128, 128)
    store = pltpu.make_async_copy(flat.at[:, pl.ds(first, count)], out, out_sem)
    store.start()
    store.wait()


def reduce_products(sources, total_rows, batches):
    step_rows = (total_rows - 8) // batches - 1
    width = step_rows + HEAD_ROWS
    return pl.pallas_call(
        reduce_kernel,
        out_shape=jax.ShapeDtypeStruct((1, (step_rows + 1) * 128), F32),
        in_specs=[any_spec()] * 5 + [vmem_spec()],
        out_specs=any_spec(),
        scratch_shapes=[
            pltpu.VMEM((4 * step_rows + HEAD_ROWS + 512, 128), BF),
            pltpu.VMEM((2, width, 128), BF),
            pltpu.VMEM((3, width, 128), BF),
            pltpu.VMEM((width // CHUNKS, 128), F32),
            pltpu.VMEM((1, width * 128), F32),
            (
                pltpu.SemaphoreType.DMA((2, CHUNKS)),
                pltpu.SemaphoreType.DMA((2, CHUNKS)),
                pltpu.SemaphoreType.DMA((2, CHUNKS)),
                pltpu.SemaphoreType.DMA((3, CHUNKS)),
                pltpu.SemaphoreType.DMA,
            ),
        ]
        + product_scratch(2 * MICRO * LEN, 2),
        compiler_params=pltpu.CompilerParams(
            collective_id=1, has_side_effects=True, vmem_limit_bytes=62 * MIB
        ),
        name="reduce_products",
    )(*sources)


def document_ids(lengths):
    ends = jnp.cumsum(lengths, axis=1)
    places = jnp.arange(LEN, dtype=jnp.int32)
    return jnp.sum((places[None, :, None] >= ends[:, None, :]).astype(jnp.int32), axis=2)


def shards(tokens, cotangent, params, lengths):
    docs = document_ids(lengths[0]).astype(F32)[:, None, :]
    batches = lax.axis_size("batch")
    paired = batches == 2 * PLACES
    acts, d_inputs, normed, middle, d_first, d_second, grads, d_gain = train(
        tokens, cotangent, params, docs, paired
    )
    total_rows = params.shape[1] // 128 + 8
    sources = (normed, d_first, d_second, middle, grads, d_gain)
    if paired:
        mine = reduce_products(sources, total_rows, batches)
    else:
        parts = products(sources, total_rows)
        mine = lax.psum_scatter(parts[8:].reshape(-1), "batch", scatter_dimension=0, tiled=True)
        mine = mine.astype(F32)[None]
    return acts[None], d_inputs[None], mine


def solution(mesh):
    return jax.shard_map(
        shards,
        mesh=mesh,
        in_specs=(P("batch", None), P("batch", None), P("section", None), P("batch", None, None)),
        out_specs=(P("section", "batch", None), P("section", "batch", None), P("section", "batch")),
        check_vma=False,
    )
```

profile of v0, /device:TPU:8, one launch (start us, length us, event | category | flops | bytes accessed | tf_op | source)
XLA Modules:
  0.0 212.4 jit_solution(14115896029856920917)
XLA Ops:
  0.6 0.9 reduce_window_sum.14
  1.5 0.1 convert_reduce_fusion
  1.6 0.6 convert_element_type.18.docs
  2.2 123.6 %train.1 = (bf16[512,1024]{1,0:T(8,128)(2,1)}, f32[512,1024]{1,0:T(8,128)}, bf16[1024,1024]{1,0:T(8,128)(2,1)}, bf16[1024,2816]{1,0:T(8,128)(2,1)}, bf16[1024,28...) custom-call(bf16[512,1024]{1,0:T(8,128)(2,1)} %tokens.1, ...), custom_call_target="tpu_custom_call" | custom-call | tf_op jit(solution)/shard_map/train/pallas_call | solution.py:662
  125.8 0.0 copy-start.1
  125.8 79.8 %reduce_products.1 = f32[1,1056896]{1,0:T(1,128)} custom-call(bf16[1024,1024]{1,0:T(8,128)(2,1)} %get-tuple-element.13.refs_0_, bf16[1024,2816]{1,0:T(8,128)(2,1)} %get-tuple-element.14.refs_1_, bf16[1024,2816]{1,0:T(8,128)(2,1)} %get-tuple-element.15.refs_2_, bf16[1024,2816]{1,0:T(8,128)(2,1)} %get-tuple-element.16.refs_3_, ...), custom_call_target="tpu_custom_call" | custom-call | tf_op jit(solution)/shard_map/reduce_products/pallas_call | solution.py:1223
  205.6 0.0 copy-done.1
  205.6 0.0 copy-start
  205.6 1.0 copy.10
  206.6 3.8 %copy.11 = f32[1,512,1024]{2,1,0:T(8,128)} copy(f32[1,512,1024]{2,1,0:T(8,128)} %bitcast.3) | data formatting | bytes 4194304
  210.4 0.0 copy-done
  210.4 2.0 copy.12
  (1 shorter events, 0.0 us)
Async XLA Ops:
  125.8 79.8 %copy-start.1 = (bf16[512,1024]{1,0:T(8,128)(2,1)S(1)}, bf16[512,1024]{1,0:T(8,128)(2,1)}, u32[]{:S(2)}) copy-start(bf16[512,1024]{1,0:T(8,128)(2,1)} %get-tuple-element.11) | copy-start | bytes 3145732
  205.6 4.8 %copy-start = (f32[1,1056896]{1,0:T(1,128)S(1)}, f32[1,1056896]{1,0:T(1,128)}, u32[]{:S(2)}) copy-start(f32[1,1056896]{1,0:T(1,128)} %reduce_products.1) | copy-start | bytes 12682756
where the time goes:
time: 213 us; the launch traced here: 212 us
  Pallas kernels  203 us (95%)
  local copies, waits for them, and re-layouts  7.41 us (3%)
    pallas_call x1, Pallas kernels, train(): pl.pallas_call(functools.partial(train_kernel, swapping), out_shape=(jax....  124 us
    pallas_call x1, Pallas kernels, reduce_products(): pl.pallas_call(reduce_kernel, out_shape=jax.ShapeDtypeStruct((1, (step_ro...  79.8 us
    unnamed x7, local copies, waits for them, and re-layouts  6.83 us

commit v1 on v0

--- a/solution.py
+++ b/solution.py
@@ -43,6 +43,18 @@
 
 def dot_0(left, right):
     return lax.dot_general(left, right, (((0,), (0,)), ((), ())), preferred_element_type=F32)
+
+
+def block256(index):
+    return pl.ds(pl.multiple_of(index * 256, 256), 256)
+
+
+def each(first, last, act):
+    def step(i, carry):
+        act(i)
+        return carry
+
+    lax.fori_loop(first, last, step, 0)
 
 
 def is_feed(section):
@@ -207,10 +219,10 @@
 
 def train_kernel(
     swapping,
-    tokens, cotangent, flat, docs,
+    tokens, cotangent, flat, lengths,
     acts, d_inputs, normed, middle, d_first, d_second, grads, d_gain,
     wide_v, tall_v, gain_v, docs_v, z_v, h_v, x_v, g_v, dz_v, first_v, second_v, mid_v, dh_v, gain_sum, far_gain,
-    raised_v, slope_v, inverse_v, mask_v, dy_v, dq_v, dk_v, dv_v, chunk, blocks, woven,
+    wide_t, tall_t, inverse_v, mask_v, dy_v, dq_v, dk_v, dv_v, chunk, blocks, woven,
     load_sem, gain_sem, in_sem, act_sem, out_sem, on_send, on_recv, back_send, back_recv, far_send, far_recv,
 ):
     section = lax.axis_index("section")
@@ -252,7 +264,14 @@
     def _():
         tangent_copy.start()
 
-    docs_v[pl.ds(0, MICRO)] = docs[...]
+    places = lax.broadcasted_iota(jnp.int32, (1, LEN), 1)
+    for micro in range(MICRO):
+        end = 0
+        ids = jnp.zeros((1, LEN), F32)
+        for document in range(lengths.shape[2]):
+            end = end + lengths[0, micro, document]
+            ids += (places >= end).astype(F32)
+        docs_v[micro] = ids
     prepare(section, flat, wide_v, tall_v, chunk, blocks, woven, load_sem)
     gain_copy.wait()
     gain = 1.0 + gain_v[...].astype(F32) / 8.0
@@ -399,6 +418,12 @@
         @pl.when(own)
         def _():
             dh_v[...] = back(rows) * SCALE
+
+            @pl.when(section < last)
+            def _():
+                hand_on(step).wait_send()
+
+            act_out(step).wait()
             z = z_v[rows, :].astype(F32)
             scaled = lax.rsqrt(jnp.mean(z * z, axis=1, keepdims=True) + EPSILON)
             unit = z * scaled
@@ -419,6 +444,26 @@
         for copy in backward_outs(phase, step):
             copy.start()
 
+    def turn_weights(low, high):
+        def wide_piece(which, t):
+            wide_t[which, block256(t), :] = wide_v[which, :, block256(t)].T
+
+        def tall_piece(t):
+            tall_t[:, block256(t)] = tall_v[block256(t), :].T
+
+        each(0, low // 256, functools.partial(wide_piece, 0))
+        each(0, high // 256, functools.partial(wide_piece, 1))
+        each(0, high // 256, tall_piece)
+
+    def kept_at(kind, index):
+        width = 2 * low_width(kind)
+        room = (FP - width) // 256 * 4
+        over = index >= room
+        place = jnp.where(over, index - room, index)
+        first = jnp.where(over, D, width) + place // 4 * 256
+        rows = pl.ds(pl.multiple_of(first, 256), 256)
+        return wide_t.at[jnp.where(over, 1, 0), rows, block256(lax.rem(place, 4))]
+
     def feed_hidden(rows):
         half = FP // 2
 
@@ -443,7 +488,7 @@
 
         def piece(part, carry):
             cols = pl.ds(pl.multiple_of(part * half, half), half)
-            d_mid = dot_t(g_v[here, :], tall_v[cols, :]) * SCALE
+            d_mid = dot(g_v[here, :], tall_t[:, cols]) * SCALE
             first_v[rows, cols] = (d_mid * first_v[rows, cols].astype(F32)).astype(BF)
             second_v[rows, cols] = (d_mid * second_v[rows, cols].astype(F32)).astype(BF)
             return carry
@@ -451,7 +496,7 @@
         lax.fori_loop(0, 2, piece, 0)
 
     def feed_back(rows):
-        return dot_t(first_v[rows, :], wide_v[0]) + dot_t(second_v[rows, :], wide_v[1])
+        return dot(first_v[rows, :], wide_t[0]) + dot(second_v[rows, :], wide_t[1])
 
     def attend_hidden(kind, phase, micro, part, rows):
         width = low_width(kind)
@@ -478,10 +523,10 @@
                 raised = jnp.exp(kept - jnp.max(kept, axis=2, keepdims=True))
             else:
                 slope = mask[None] * (1.0 + scores)
-                slope_v[step, t, :, cols] = slope.astype(BF).reshape(2 * ROWS, span)
+                kept_at(kind, (steps + step) * 8 + t)[:, cols] = slope.astype(BF).reshape(2 * ROWS, span)
                 raised = 0.5 * (mask[None] + slope * slope)
             raised = raised.astype(BF).reshape(2 * ROWS, span)
-            raised_v[step, t, :, cols] = raised
+            kept_at(kind, step * 8 + t)[:, cols] = raised
             summed = dot(raised, jnp.concatenate([values, jnp.ones((span, 128), BF)], axis=1))
             inverse = 1.0 / summed[:, 128:]
             sides = [lanes_of_value(half) for half in range(2)]
@@ -500,7 +545,7 @@
         keys_at = pl.ds(pl.multiple_of(micro * LEN, LEN), span)
         own = pl.ds(0, span)
         step = micro * CHUNKS_OF + part
-        d_mixed = dot_t(g_v[here, :], tall_v[pl.ds(0, D), :]) * out_scale(kind)
+        d_mixed = dot(g_v[here, :], tall_t[:, pl.ds(0, D)]) * out_scale(kind)
         dy_v[...] = (d_mixed * inverse_v[rows, :]).astype(BF)
         if part == CHUNKS_OF - 1:
             dk_v[...] = jnp.zeros_like(dk_v)
@@ -519,8 +564,8 @@
             mixed = mid_v[rows, block_of(t)].astype(F32)
             shift = jnp.sum(d_mixed.astype(F32) * jnp.concatenate([mixed, mixed], axis=0), axis=1, keepdims=True)
             d_weights = dot_t(d_mixed, values) - shift
-            raised = raised_v[step, t, :, own]
-            slope = raised if kind == WINDOW else slope_v[step, t, :, own]
+            raised = kept_at(kind, step * 8 + t)[:, own]
+            slope = raised if kind == WINDOW else kept_at(kind, (steps + step) * 8 + t)[:, own]
             d_scores = (slope.astype(F32) * d_weights).astype(BF)
             dv_v[own, block_of(t)] += dot_0(raised, d_mixed)
             d_queries = merge(heads, dot(d_scores, keys)) * root_of(kind)
@@ -539,20 +584,41 @@
 
     def attend_back(kind, rows):
         width = low_width(kind)
-        total = dot_t(first_v[rows, pl.ds(0, 2 * width)], wide_v[0, :, pl.ds(0, 2 * width)])
-        total += dot_t(second_v[rows, pl.ds(0, D)], wide_v[1, :, pl.ds(0, D)])
+        total = dot(first_v[rows, pl.ds(0, 2 * width)], wide_t[0, pl.ds(0, 2 * width), :])
+        total += dot(second_v[rows, pl.ds(0, D)], wide_t[1, pl.ds(0, D), :])
         return total
+
+    @pl.when(section == last)
+    def _():
+        turn_weights(FP, FP)
+
+    @pl.when(section == WINDOW)
+    def _():
+        turn_weights(2 * D, D)
 
     def one_phase(phase, carry):
         own = phase == 0
 
         @pl.when(is_feed(section))
         def _():
-            def forward(step, inner):
-                forward_step(phase, step, feed_hidden, feed_project)
-                return inner
-
-            lax.fori_loop(0, steps, forward, 0)
+            turns = jnp.where(own & (section == last), MICRO, 1)
+            span = steps // turns
+
+            def backward(step):
+                micro, part = step // CHUNKS_OF, CHUNKS_OF - 1 - lax.rem(step, CHUNKS_OF)
+                backward_step(phase, micro * CHUNKS_OF + part, feed_unhidden, feed_back)
+
+            def turn(index):
+                here = (index * span, index * span + span)
+                each(*here, lambda step: forward_step(phase, step, feed_hidden, feed_project))
+
+                @pl.when(own & (section < last))
+                def _():
+                    turn_weights(FP, FP)
+
+                each(*here, backward)
+
+            each(0, turns, turn)
 
         for kind in (WINDOW, LINEAR):
 
@@ -570,30 +636,6 @@
 
                 lax.fori_loop(0, MICRO, forward, 0)
 
-        def settle(step, inner):
-            @pl.when(own)
-            def _():
-                @pl.when(section < last)
-                def _():
-                    hand_on(step).wait_send()
-
-                act_out(step).wait()
-
-            for copy in forward_outs(phase, step):
-                copy.wait()
-            return inner
-
-        lax.fori_loop(0, steps, settle, 0)
-
-        @pl.when(is_feed(section))
-        def _():
-            def backward(step, inner):
-                micro, part = step // CHUNKS_OF, CHUNKS_OF - 1 - lax.rem(step, CHUNKS_OF)
-                backward_step(phase, micro * CHUNKS_OF + part, feed_unhidden, feed_back)
-                return inner
-
-            lax.fori_loop(0, steps, backward, 0)
-
         for kind in (WINDOW, LINEAR):
 
             @pl.when(section == kind)
@@ -608,6 +650,8 @@
                         )
                     return inner
 
+                if kind == LINEAR:
+                    turn_weights(2 * low_width(kind), D)
                 lax.fori_loop(0, MICRO, backward, 0)
 
         @pl.when(own & gives)
@@ -623,7 +667,7 @@
 
                 gradient_out(step).wait()
 
-            for copy in backward_outs(phase, step):
+            for copy in forward_outs(phase, step) + backward_outs(phase, step):
                 copy.wait()
             return inner
 
@@ -655,7 +699,7 @@
 UNROLL = 2
 
 
-def train(tokens, cotangent, flat, docs, swapping):
+def train(tokens, cotangent, flat, lengths, swapping):
     count = MICRO * LEN
     steps = MICRO * CHUNKS_OF
     kept = 2 * count if swapping else count
@@ -671,7 +715,7 @@
             jax.ShapeDtypeStruct((kept, D), BF),
             jax.ShapeDtypeStruct((8, D), F32),
         ),
-        in_specs=[any_spec()] * 3 + [vmem_spec()],
+        in_specs=[any_spec()] * 3 + [pl.BlockSpec(memory_space=pltpu.SMEM)],
         out_specs=(any_spec(),) * 7 + (vmem_spec(),),
         scratch_shapes=[
             pltpu.VMEM((2, D, FP), BF),
@@ -689,8 +733,8 @@
             pltpu.VMEM((ROWS, D), F32),
             pltpu.VMEM((8, D), F32),
             pltpu.VMEM((8, D), F32),
-            pltpu.VMEM((steps, 8, 2 * ROWS, LEN), BF),
-            pltpu.VMEM((steps, 8, 2 * ROWS, LEN), BF),
+            pltpu.VMEM((2, FP, D), BF),
+            pltpu.VMEM((D, FP), BF),
             pltpu.VMEM((count, D), F32),
             pltpu.VMEM((ROWS, LEN), F32),
             pltpu.VMEM((ROWS, D), BF),
@@ -716,11 +760,13 @@
             collective_id=0, has_side_effects=True, vmem_limit_bytes=62 * MIB
         ),
         name="train",
-    )(tokens, cotangent, flat, docs)
+    )(tokens, cotangent, flat, lengths)
 
 
 HEAD_ROWS = 16
-PAIR_ROWS = 128 * 43
+PAIRS = 64
+PAIR_ROWS = PAIRS * 43
+PAIR_TILES = D // 2 // PAIRS
 CHUNKS = 11
 
 
@@ -774,7 +820,7 @@
         lax.fori_loop(0, rows // piece, step, 0)
 
     def pairs(self, which, first_pair):
-        count = 128
+        count = PAIRS
         stage, woven = self.stage, self.woven
         half = FP // 2
         low_half = lax.broadcasted_iota(jnp.int32, (count, 128), 1) < 64
@@ -792,7 +838,7 @@
             before = here
 
     def pair_tile(self, out, k, tail_only):
-        self.pairs(k // 4, lax.rem(k, 4) * 128)
+        self.pairs(k // PAIR_TILES, lax.rem(k, PAIR_TILES) * PAIRS)
 
         @pl.when(jnp.logical_not(tail_only))
         def _():
@@ -833,26 +879,18 @@
         self.tall(out, left, right, 8, 512, HEAD_ROWS + 4096 * (k + 1), scale, 512)
 
 
-DOWN_ROW = HEAD_ROWS + 8 * PAIR_ROWS
+DOWN_ROW = HEAD_ROWS + 2 * PAIR_TILES * PAIR_ROWS
 DOWN_TILES = FP // 256
 WINDOW_END = HEAD_ROWS + 4 * 8192
 LINEAR_END = HEAD_ROWS + 20480
-
-
-def each(first, last, act):
-    def step(i, carry):
-        act(i)
-        return carry
-
-    lax.fori_loop(first, last, step, 0)
 
 
 def product_scratch(count, slots):
     return [
         pltpu.VMEM((2, count, D), BF),
         pltpu.VMEM((slots, count, FP), BF),
-        pltpu.VMEM((22, 256, 128), F32),
-        pltpu.VMEM((6144, 128), F32),
+        pltpu.VMEM((22, 2 * PAIRS, 128), F32),
+        pltpu.VMEM((4096, 128), F32),
         pltpu.SemaphoreType.DMA((5,)),
     ]
 
@@ -883,7 +921,7 @@
     @pl.when(is_feed(section))
     def _():
         load("h", "g", "first", "second", "middle")
-        each(0, 8, lambda k: work.pair_tile(out_v, k, section < 0))
+        each(0, 2 * PAIR_TILES, lambda k: work.pair_tile(out_v, k, section < 0))
         each(0, DOWN_TILES, lambda j: work.down_tile(out_v, j))
 
     for kind in (WINDOW, LINEAR):
@@ -941,8 +979,9 @@
     pair_here = feed_here | window_here
     linear_here = section == LINEAR
     sets = (
-        (feed_here & (place < 2), ("h", "first", "second")),
-        (feed_here & (place >= 2), ("h", "second", "middle", "g")),
+        (feed_here & (place < 2), ("h", "first")),
+        (feed_here & (place == 2), ("middle", "g")),
+        (feed_here & (place == 3), ("h", "second")),
         (window_here, ("all_h", "all_mixed", "all_low", "all_value", "all_g")),
         (linear_here, ("some_h", "some_mixed", "some_low", "some_value", "some_g")),
     )
@@ -974,6 +1013,22 @@
         def _(names=names):
             for copy in work.loads(names):
                 copy.wait()
+
+    late_sets = (
+        (feed_here & (place < 2), ("second",)),
+        (feed_here & (place == 2), ("h", "second")),
+        (feed_here & (place == 3), ("middle", "g")),
+    )
+
+    def late(act):
+        for here, names in late_sets:
+
+            @pl.when(here)
+            def _(names=names):
+                for copy in work.loads(names):
+                    act(copy)
+
+    late(lambda copy: copy.start())
 
     def rows_of(i):
         return pl.ds(pl.multiple_of(i * piece, 16), piece)
@@ -1045,6 +1100,15 @@
     def swapped(to, limits=(CHUNKS, CHUNKS)):
         each(0, jnp.where(core == 0, limits[1], limits[0]), lambda i: swap(to, i).wait_send())
 
+    def store(which):
+        rows = out.shape[1] // 128
+        early = (CHUNKS - 1) * piece - 32
+        begin, size = ((0, early), (early, rows - early))[which]
+        source = pl.ds(pl.multiple_of((8 + batch + begin) * 128, 128), size * 128)
+        return pltpu.make_async_copy(
+            flat.at[:, source], out.at[:, pl.ds(begin * 128, size * 128)], out_sem.at[which]
+        )
+
     def emit(i):
         cols = pl.ds(pl.multiple_of(i * piece * 128, 1024), piece * 128)
         flat[0:1, cols] = total[...].reshape(1, piece * 128)
@@ -1054,18 +1118,31 @@
     @pl.when(feed_here)
     def _():
         upper = place >= 2
+        share_tiles = 2 * step_rows // PAIR_ROWS
+        upper_tiles = 2 * PAIR_TILES - 2 * share_tiles
 
         def pair(t):
-            k = jnp.where(upper, 5 + t, lax.rem(t + jnp.where(place == 0, 2, 0), 6))
-            tail_only = upper & (t == 0)
+            turned = jnp.where(t < share_tiles, t + share_tiles, jnp.where(t == share_tiles, share_tiles - 1, t - share_tiles - 1))
+            k = jnp.where(place == 0, turned, t)
+            k = jnp.where(upper, jnp.where(t == upper_tiles, 2 * share_tiles - 1, 2 * share_tiles + t), k)
+            tail_only = upper & (t == upper_tiles)
+
+            @pl.when(jnp.logical_not(upper) & (k == PAIR_TILES))
+            def _():
+                late(lambda copy: copy.wait())
+
             work.pair_tile(part, k, tail_only)
             start = HEAD_ROWS + PAIR_ROWS * k - base
             stop = start + PAIR_ROWS
-            early = jnp.where(k == 1, whole, jnp.where(k < 1, stop, start))
-            stop_0 = jnp.where(place == 0, early, stop)
+            ends_late = (place == 0) & (k == share_tiles - 1)
             to = base // (2 * step_rows)
-            release(to, jnp.where(tail_only, 0, start), jnp.where(tail_only, 0, stop_0))
-            release(to + 1, start - 2 * step_rows, stop - 2 * step_rows)
+            early = jnp.where(k == share_tiles - 2, whole, jnp.where(k < share_tiles - 2, stop, start))
+            before_0 = jnp.where(tail_only, 0, jnp.where(upper & (k == 2 * share_tiles), piece, start))
+            after_0 = jnp.where(tail_only, piece, jnp.where(place == 0, early, stop))
+            release(to, before_0, after_0)
+            before_1 = jnp.where(ends_late, 0, jnp.where((place == 0) & (k == share_tiles), piece, start - 2 * step_rows))
+            after_1 = jnp.where(ends_late, piece, stop - 2 * step_rows)
+            release(to + 1, before_1, after_1)
 
         def down(j):
             work.down_tile(part, j)
@@ -1078,7 +1155,15 @@
         def turn(t):
             @pl.when(t == 1)
             def _():
-                each(0, jnp.where(upper, 3, 6), pair)
+                @pl.when(place == 2)
+                def _():
+                    late(lambda copy: copy.wait())
+
+                each(0, jnp.where(upper, upper_tiles + 1, 2 * share_tiles), pair)
+
+                @pl.when(place == 3)
+                def _():
+                    late(lambda copy: copy.wait())
 
             mate_first = place == 2
             first = jnp.where(mate_first & (t == 0), 2, 0)
@@ -1173,15 +1258,22 @@
                 both_ways = passing[1, rows, :].astype(F32) + passing[2, rows, :].astype(F32)
                 total[...] = own[1, rows, :].astype(F32) + both_ways
 
-            here = jnp.where(place == 0, own_count(0), jnp.where(place == 1, own_count(1), 0))
-
-            @pl.when(i >= here)
-            def _():
-                total[...] = jnp.zeros_like(total)
-
             emit(i)
 
-        each(0, CHUNKS, sum_up)
+        here = jnp.where(place == 0, own_count(0), jnp.where(place == 1, own_count(1), 0))
+        total[...] = jnp.zeros_like(total)
+        each(here, CHUNKS, emit)
+        each(0, here - 1, sum_up)
+
+        @pl.when(here == CHUNKS)
+        def _():
+            store(0).start()
+
+        each(jnp.maximum(here - 1, 0), here, sum_up)
+
+        @pl.when(here < CHUNKS)
+        def _():
+            store(0).start()
 
         @pl.when((place == 1) | (place >= 2))
         def _():
@@ -1195,6 +1287,7 @@
     def _():
         total[...] = jnp.zeros_like(total)
         each(0, CHUNKS, emit)
+        store(0).start()
 
     @pl.when(pair_here)
     def _():
@@ -1206,15 +1299,15 @@
             total[...] = own[slot, rows, :].astype(F32) + passing[0, rows, :].astype(F32)
             emit(i)
 
-        each(0, CHUNKS, sum_up)
+        each(0, CHUNKS - 1, sum_up)
+        store(0).start()
+        each(CHUNKS - 1, CHUNKS, sum_up)
         other = 2 * mate + core
         each(0, CHUNKS, lambda i: go(passing.at[0, rows_of(i), :], 0, mate, i, other).wait_send())
 
-    count = out.shape[1]
-    first = pl.multiple_of((8 + batch) * 128, 128)
-    store = pltpu.make_async_copy(flat.at[:, pl.ds(first, count)], out, out_sem)
-    store.start()
-    store.wait()
+    store(1).start()
+    store(0).wait()
+    store(1).wait()
 
 
 def reduce_products(sources, total_rows, batches):
@@ -1236,29 +1329,22 @@
                 pltpu.SemaphoreType.DMA((2, CHUNKS)),
                 pltpu.SemaphoreType.DMA((2, CHUNKS)),
                 pltpu.SemaphoreType.DMA((3, CHUNKS)),
-                pltpu.SemaphoreType.DMA,
+                pltpu.SemaphoreType.DMA((2,)),
             ),
         ]
         + product_scratch(2 * MICRO * LEN, 2),
         compiler_params=pltpu.CompilerParams(
-            collective_id=1, has_side_effects=True, vmem_limit_bytes=62 * MIB
+            collective_id=1, has_side_effects=True, vmem_limit_bytes=60 * MIB
         ),
         name="reduce_products",
     )(*sources)
 
 
-def document_ids(lengths):
-    ends = jnp.cumsum(lengths, axis=1)
-    places = jnp.arange(LEN, dtype=jnp.int32)
-    return jnp.sum((places[None, :, None] >= ends[:, None, :]).astype(jnp.int32), axis=2)
-
-
 def shards(tokens, cotangent, params, lengths):
-    docs = document_ids(lengths[0]).astype(F32)[:, None, :]
     batches = lax.axis_size("batch")
     paired = batches == 2 * PLACES
     acts, d_inputs, normed, middle, d_first, d_second, grads, d_gain = train(
-        tokens, cotangent, params, docs, paired
+        tokens, cotangent, params, lengths, paired
     )
     total_rows = params.shape[1] // 128 + 8
     sources = (normed, d_first, d_second, middle, grads, d_gain)

time: 213 us -> 195 us (0.915)
  Pallas kernels: 203 us -> 189 us
    pallas_call x1, Pallas kernels: 124 us -> 110 us  [train(): pl.pallas_call(functools.partial(train_kernel, swapping), out_shape=(jax....]
    unnamed x7 -> x9, local copies, waits for them, and re-layouts: 6.83 us -> 5.35 us
where the time goes in v1:
time: 195 us
  Pallas kernels  189 us (97%)
  local copies, waits for them, and re-layouts  5.35 us (3%)
    pallas_call x1, Pallas kernels, train(): pl.pallas_call(functools.partial(train_kernel, swapping), out_shape=(jax....  110 us
    pallas_call x1, Pallas kernels, reduce_products(): pl.pallas_call(reduce_kernel, out_shape=jax.ShapeDtypeStruct((1, (step_ro...  79.4 us
    unnamed x9, local copies, waits for them, and re-layouts  5.35 us

profile of v1, /device:TPU:8, one launch (start us, length us, event | category | flops | bytes accessed | tf_op | source)
XLA Modules:
  0.0 195.0 jit_solution(15443745036463573424)
XLA Ops:
  0.6 109.6 %train.1 = (bf16[512,1024]{1,0:T(8,128)(2,1)}, f32[512,1024]{1,0:T(8,128)}, bf16[1024,1024]{1,0:T(8,128)(2,1)}, bf16[1024,2816]{1,0:T(8,128)(2,1)}, bf16[1024,28...) custom-call(bf16[512,1024]{1,0:T(8,128)(2,1)} %tokens.1, ...), custom_call_target="tpu_custom_call" | custom-call | tf_op jit(solution)/shard_map/train/pallas_call | solution.py:706
  110.3 0.0 copy-start.2
  110.3 0.0 copy-start.1
  110.3 79.4 %reduce_products.1 = f32[1,1056896]{1,0:T(1,128)} custom-call(bf16[1024,1024]{1,0:T(8,128)(2,1)} %get-tuple-element.13.refs_0_, bf16[1024,2816]{1,0:T(8,128)(2,1)} %get-tuple-element.14.refs_1_, bf16[1024,2816]{1,0:T(8,128)(2,1)} %get-tuple-element.15.refs_2_, bf16[1024,2816]{1,0:T(8,128)(2,1)} %get-tuple-element.16.refs_3_, ...), custom_call_target="tpu_custom_call" | custom-call | tf_op jit(solution)/shard_map/reduce_products/pallas_call | solution.py:1316
  189.7 0.0 copy-done.2
  189.7 0.0 copy-start
  189.7 1.0 copy.10
  190.6 0.0 copy-done.1
  190.7 1.3 copy.11
  192.0 1.0 copy-done
  193.0 2.0 %copy.12 = f32[1,1056896]{1,0:T(1,128)} copy(f32[1,1056896]{1,0:T(1,128)S(1)} %copy-done) | data formatting | bytes 8455168
Async XLA Ops:
  110.3 79.4 %copy-start.2 = (bf16[512,1024]{1,0:T(8,128)(2,1)S(1)}, bf16[512,1024]{1,0:T(8,128)(2,1)}, u32[]{:S(2)}) copy-start(bf16[512,1024]{1,0:T(8,128)(2,1)} %get-tuple-element.11) | copy-start | bytes 3145732
  110.3 80.4 %copy-start.1 = (f32[512,1024]{1,0:T(8,128)S(1)}, f32[512,1024]{1,0:T(8,128)}, u32[]{:S(2)}) copy-start(f32[512,1024]{1,0:T(8,128)} %get-tuple-element.12) | copy-start | bytes 6291460
  189.7 3.3 %copy-start = (f32[1,1056896]{1,0:T(1,128)S(1)}, f32[1,1056896]{1,0:T(1,128)}, u32[]{:S(2)}) copy-start(f32[1,1056896]{1,0:T(1,128)} %reduce_products.1) | copy-start | bytes 12682756

commit v2 on v1

--- a/solution.py
+++ b/solution.py
@@ -63,7 +63,7 @@
 
 PAIR_STEP = 32 * FF
 ROW_STEP = 64 * D
-AHEAD = 8
+AHEAD = 12
 
 
 def prepare(section, flat, wide_v, tall_v, chunk, blocks, woven, load_sem):
@@ -796,6 +796,8 @@
             table[prefix + "mixed"] = (self.middle.at[rows, low], self.left_v.at[1, rows, :], 1)
             table[prefix + "low"] = (self.d_first.at[rows, both], self.d_v.at[0, rows, both], 2)
             table[prefix + "value"] = (self.d_second.at[rows, low], self.d_v.at[1, rows, low], 3)
+            few = pl.ds(0, 2 * HEADS * FEAT)
+            table["few_low"] = (self.d_first.at[some, few], self.d_v.at[0, some, few], 2)
             table[prefix + "g"] = (self.grads.at[rows, :], self.d_v.at[1, rows, high], 4)
         return [self.fetch(*table[name]) for name in names]
 
@@ -982,8 +984,9 @@
         (feed_here & (place < 2), ("h", "first")),
         (feed_here & (place == 2), ("middle", "g")),
         (feed_here & (place == 3), ("h", "second")),
-        (window_here, ("all_h", "all_mixed", "all_low", "all_value", "all_g")),
-        (linear_here, ("some_h", "some_mixed", "some_low", "some_value", "some_g")),
+        (window_here & (place == 0), ("all_h", "all_value")),
+        (window_here & (place == 1), ("all_h", "all_low")),
+        (linear_here, ("some_h", "few_low")),
     )
     for here, names in sets:
 
@@ -1018,6 +1021,9 @@
         (feed_here & (place < 2), ("second",)),
         (feed_here & (place == 2), ("h", "second")),
         (feed_here & (place == 3), ("middle", "g")),
+        (window_here & (place == 0), ("all_mixed", "all_g", "all_low")),
+        (window_here & (place == 1), ("all_value", "all_mixed", "all_g")),
+        (linear_here, ("some_mixed", "some_value", "some_g")),
     )
 
     def late(act):
@@ -1062,40 +1068,32 @@
         pltpu.make_async_copy(here, here, recv.at[slot, i]).wait()
 
     def release(to, before, after, limits=(CHUNKS, CHUNKS)):
-        for parity in range(2):
-
-            def bound(row, parity=parity):
-                return jnp.minimum(jnp.maximum(row - parity * step_rows, 0) // piece, limits[parity])
-
-            first, last = bound(before), bound(after)
-
-            @pl.when(core != parity)
-            def _(first=first, last=last):
-                each(first, last, lambda i: swap(to, i).start())
-
-            def add(i):
-                slot = lax.rem(to, 2)
-                rows = rows_of(i)
-                swap(to, i).wait_recv()
-                mine = part[share(2 * to + core, i), :].astype(F32)
-                own[slot, rows, :] = (own[slot, rows, :].astype(F32) + mine).astype(BF)
-                source = own.at[slot, rows, :]
-
-                @pl.when(pair_here & (to == mate))
-                def _():
-                    go(source, 0, to, i, 2 * mate + core).start()
-
-                @pl.when(linear_here & (place == PLACES - 1))
-                def _():
-                    go(source, slot, to, i, batch - 2).start()
-
-                @pl.when(linear_here & (place == 0) & (to == 1))
-                def _():
-                    go(source, 2, to, i, batch + 2).start()
-
-            @pl.when(core == parity)
-            def _(first=first, last=last):
-                each(first, last, add)
+        def bound(row, parity):
+            most = jnp.where(parity == 0, limits[0], limits[1])
+            return jnp.minimum(jnp.maximum(row - parity * step_rows, 0) // piece, most)
+
+        def add(i):
+            slot = lax.rem(to, 2)
+            rows = rows_of(i)
+            swap(to, i).wait_recv()
+            mine = part[share(2 * to + core, i), :].astype(F32)
+            own[slot, rows, :] = (own[slot, rows, :].astype(F32) + mine).astype(BF)
+            source = own.at[slot, rows, :]
+
+            @pl.when(pair_here & (to == mate))
+            def _():
+                go(source, 0, to, i, 2 * mate + core).start()
+
+            @pl.when(linear_here & (place == PLACES - 1))
+            def _():
+                go(source, slot, to, i, batch - 2).start()
+
+            @pl.when(linear_here & (place == 0) & (to == 1))
+            def _():
+                go(source, 2, to, i, batch + 2).start()
+
+        each(bound(before, 1 - core), bound(after, 1 - core), lambda i: swap(to, i).start())
+        each(bound(before, core), bound(after, core), add)
 
     def swapped(to, limits=(CHUNKS, CHUNKS)):
         each(0, jnp.where(core == 0, limits[1], limits[0]), lambda i: swap(to, i).wait_send())
@@ -1179,6 +1177,11 @@
     def _():
         def tile(t, carry):
             k = lax.rem(t + jnp.where(place == 0, 4, 0), 8)
+
+            @pl.when(t == jnp.where(place == 0, 2, 4))
+            def _():
+                late(lambda copy: copy.wait())
+
             work.window_tile(part, k)
             start = HEAD_ROWS + 4096 * k
             stop = start + 4096
@@ -1216,29 +1219,33 @@
             release(0, start, stop, limits[0])
             release(1, start - 2 * step_rows, stop - 2 * step_rows, limits[1])
 
+        def pass_on(to, i):
+            rows = rows_of(i)
+            arrived(to, i)
+            added = passing[to, rows, :].astype(F32) + own[to, rows, :].astype(F32)
+            passing[to, rows, :] = added.astype(BF)
+            go(passing.at[to, rows, :], to, to, i, batch - 2).start()
+
+        ahead = jnp.where((place == 2) & (core == 0), 2, 0)
+
+        def value_and_on(k):
+            value(k)
+            each(jnp.minimum(jnp.maximum(k - 1, 0), ahead), jnp.minimum(k, ahead), functools.partial(pass_on, 0))
+
         each(0, 2, low)
-        each(0, 4, value)
+        late(lambda copy: copy.wait())
+        each(0, 4, value_and_on)
 
         def own_count(to):
             return jnp.where(core == 0, limits[to][0], limits[to][1])
 
-        def pass_down(to):
-            def act(i):
-                rows = rows_of(i)
-                arrived(to, i)
-                added = passing[to, rows, :].astype(F32) + own[to, rows, :].astype(F32)
-                passing[to, rows, :] = added.astype(BF)
-                go(passing.at[to, rows, :], to, to, i, batch - 2).start()
-
-            each(0, own_count(to), act)
-
         @pl.when((place == 1) | (place == 2))
         def _():
-            pass_down(0)
+            each(ahead, own_count(0), functools.partial(pass_on, 0))
 
         @pl.when(place == 2)
         def _():
-            pass_down(1)
+            each(0, own_count(1), functools.partial(pass_on, 1))
 
         for to in range(2):
             swapped(to, limits[to])

time: 195 us -> 190 us (0.974)
  Pallas kernels: 189 us -> 184 us
    pallas_call x1, Pallas kernels: 79.4 us -> 75 us  [reduce_products(): pl.pallas_call(reduce_kernel, out_shape=jax.ShapeDtypeStruct((1, (step_ro...]
where the time goes in v2:
time: 190 us
  Pallas kernels  184 us (97%)
  local copies, waits for them, and re-layouts  5.35 us (3%)
    pallas_call x1, Pallas kernels, train(): pl.pallas_call(functools.partial(train_kernel, swapping), out_shape=(jax....  109 us
    pallas_call x1, Pallas kernels, reduce_products(): pl.pallas_call(reduce_kernel, out_shape=jax.ShapeDtypeStruct((1, (step_ro...  75 us
    unnamed x9, local copies, waits for them, and re-layouts  5.35 us

profile of v2, /device:TPU:8, one launch (start us, length us, event | category | flops | bytes accessed | tf_op | source)
XLA Modules:
  0.0 189.6 jit_solution(6172617740410268929)
XLA Ops:
  0.6 108.5 %train.1 = (bf16[512,1024]{1,0:T(8,128)(2,1)}, f32[512,1024]{1,0:T(8,128)}, bf16[1024,1024]{1,0:T(8,128)(2,1)}, bf16[1024,2816]{1,0:T(8,128)(2,1)}, bf16[1024,28...) custom-call(bf16[512,1024]{1,0:T(8,128)(2,1)} %tokens.1, ...), custom_call_target="tpu_custom_call" | custom-call | tf_op jit(solution)/shard_map/train/pallas_call | solution.py:706
  109.2 0.0 copy-start.2
  109.2 0.0 copy-start.1
  109.2 75.0 %reduce_products.1 = f32[1,1056896]{1,0:T(1,128)} custom-call(bf16[1024,1024]{1,0:T(8,128)(2,1)} %get-tuple-element.13.refs_0_, bf16[1024,2816]{1,0:T(8,128)(2,1)} %get-tuple-element.14.refs_1_, bf16[1024,2816]{1,0:T(8,128)(2,1)} %get-tuple-element.15.refs_2_, bf16[1024,2816]{1,0:T(8,128)(2,1)} %get-tuple-element.16.refs_3_, ...), custom_call_target="tpu_custom_call" | custom-call | tf_op jit(solution)/shard_map/reduce_products/pallas_call | solution.py:1323
  184.2 0.0 copy-done.2
  184.2 0.0 copy-start
  184.2 1.0 copy.10
  185.2 0.0 copy-done.1
  185.2 1.3 copy.11
  186.5 1.0 copy-done
  187.5 2.0 %copy.12 = f32[1,1056896]{1,0:T(1,128)} copy(f32[1,1056896]{1,0:T(1,128)S(1)} %copy-done) | data formatting | bytes 8455168
Async XLA Ops:
  109.2 75.0 %copy-start.2 = (bf16[512,1024]{1,0:T(8,128)(2,1)S(1)}, bf16[512,1024]{1,0:T(8,128)(2,1)}, u32[]{:S(2)}) copy-start(bf16[512,1024]{1,0:T(8,128)(2,1)} %get-tuple-element.11) | copy-start | bytes 3145732
  109.2 76.0 %copy-start.1 = (f32[512,1024]{1,0:T(8,128)S(1)}, f32[512,1024]{1,0:T(8,128)}, u32[]{:S(2)}) copy-start(f32[512,1024]{1,0:T(8,128)} %get-tuple-element.12) | copy-start | bytes 6291460
  184.2 3.3 %copy-start = (f32[1,1056896]{1,0:T(1,128)S(1)}, f32[1,1056896]{1,0:T(1,128)}, u32[]{:S(2)}) copy-start(f32[1,1056896]{1,0:T(1,128)} %reduce_products.1) | copy-start | bytes 12682756

commit v3 on v2

--- a/solution.py
+++ b/solution.py
@@ -467,8 +467,8 @@
     def feed_hidden(rows):
         half = FP // 2
 
-        def piece(part, carry):
-            cols = pl.ds(pl.multiple_of(part * half, half), half)
+        for part in range(2):
+            cols = pl.ds(part * half, half)
             gate = dot(h_v[rows, :], wide_v[0, :, cols]) * SCALE
             up = dot(h_v[rows, :], wide_v[1, :, cols]) * SCALE
             sig = 1.0 / (1.0 + jnp.exp(-gate))
@@ -476,9 +476,6 @@
             first_v[rows, cols] = (up * (sig + silu * (1.0 - sig))).astype(BF)
             second_v[rows, cols] = silu.astype(BF)
             mid_v[rows, cols] = (silu * up).astype(BF)
-            return carry
-
-        lax.fori_loop(0, 2, piece, 0)
 
     def feed_project(rows):
         return dot(mid_v[rows, :], tall_v[...]) * SCALE
@@ -486,14 +483,11 @@
     def feed_unhidden(here, rows):
         half = FP // 2
 
-        def piece(part, carry):
-            cols = pl.ds(pl.multiple_of(part * half, half), half)
+        for part in range(2):
+            cols = pl.ds(part * half, half)
             d_mid = dot(g_v[here, :], tall_t[:, cols]) * SCALE
             first_v[rows, cols] = (d_mid * first_v[rows, cols].astype(F32)).astype(BF)
             second_v[rows, cols] = (d_mid * second_v[rows, cols].astype(F32)).astype(BF)
-            return carry
-
-        lax.fori_loop(0, 2, piece, 0)
 
     def feed_back(rows):
         return dot(first_v[rows, :], wide_t[0]) + dot(second_v[rows, :], wide_t[1])
@@ -696,7 +690,7 @@
         far_copy(3).wait_send()
 
 
-UNROLL = 2
+UNROLL = 4
 
 
 def train(tokens, cotangent, flat, lengths, swapping):
@@ -862,10 +856,11 @@
         self.tall(out, left, self.left_v[1], 8, 256, DOWN_ROW + 2048 * j, SCALE, 512)
 
     def window_tile(self, out, k):
-        left = self.left_v[k // 6, :, pl.ds(pl.multiple_of(lax.rem(k, 2) * 512, 512), 512)]
-        right = self.d_v[k // 4, :, pl.ds(pl.multiple_of(lax.rem(k // 2, 2) * D, D), D)]
-        scale = jnp.where(k < 6, SCALE, out_scale(WINDOW))
-        self.tall(out, left, right, 8, 512, HEAD_ROWS + 4096 * k, scale, 512)
+        which = k // 4
+        left = self.left_v[which // 3, :, block256(lax.rem(k, 4))]
+        right = self.d_v[which // 2, :, pl.ds(pl.multiple_of(lax.rem(which, 2) * D, D), D)]
+        scale = jnp.where(which < 3, SCALE, out_scale(WINDOW))
+        self.tall(out, left, right, 8, 256, HEAD_ROWS + 2048 * k, scale, 512)
 
     def low_tile(self, out, k):
         some = pl.ds(0, MICRO * LEN)
@@ -932,7 +927,7 @@
         def _(kind=kind):
             load("some_h", "some_mixed", "some_low", "some_value", "some_g")
             if kind == WINDOW:
-                each(0, 8, lambda k: work.window_tile(out_v, k))
+                each(0, 16, lambda k: work.window_tile(out_v, k))
             else:
                 each(0, 2, lambda k: work.low_tile(out_v, k))
                 each(0, 4, lambda k: work.value_tile(out_v, k))
@@ -1176,27 +1171,27 @@
     @pl.when(window_here)
     def _():
         def tile(t, carry):
-            k = lax.rem(t + jnp.where(place == 0, 4, 0), 8)
-
-            @pl.when(t == jnp.where(place == 0, 2, 4))
+            k = lax.rem(t + jnp.where(place == 0, 8, 0), 16)
+
+            @pl.when(t == jnp.where(place == 0, 4, 8))
             def _():
                 late(lambda copy: copy.wait())
 
             work.window_tile(part, k)
-            start = HEAD_ROWS + 4096 * k
-            stop = start + 4096
-
-            @pl.when(k == 7)
+            start = HEAD_ROWS + 2048 * k
+            stop = start + 2048
+
+            @pl.when(k == 15)
             def _():
                 clear(part, WINDOW_END, 4 * step_rows + HEAD_ROWS - WINDOW_END)
 
-            stop_0 = jnp.where(place == 0, jnp.where(k < 3, stop, jnp.where(k == 3, whole, start)), stop)
-            stop_1 = jnp.where(k == 7, whole, stop - 2 * step_rows)
+            stop_0 = jnp.where(place == 0, jnp.where(k < 7, stop, jnp.where(k == 7, whole, start)), stop)
+            stop_1 = jnp.where(k == 15, whole, stop - 2 * step_rows)
             release(0, start, stop_0)
             release(1, start - 2 * step_rows, stop_1)
             return carry
 
-        lax.fori_loop(0, 8, tile, 0)
+        lax.fori_loop(0, 16, tile, 0)
         for to in range(2):
             swapped(to)
 

time: 190 us -> 188 us (0.989)
  Pallas kernels: 184 us -> 180 us
    pallas_call x1, Pallas kernels: 109 us -> 105 us  [train(): pl.pallas_call(functools.partial(train_kernel, swapping), out_shape=(jax....]
where the time goes in v3:
time: 188 us; the launch traced here: 186 us
  Pallas kernels  180 us (96%)
  local copies, waits for them, and re-layouts  5.35 us (3%)
    pallas_call x1, Pallas kernels, train(): pl.pallas_call(functools.partial(train_kernel, swapping), out_shape=(jax....  105 us
    pallas_call x1, Pallas kernels, reduce_products(): pl.pallas_call(reduce_kernel, out_shape=jax.ShapeDtypeStruct((1, (step_ro...  74.9 us
    unnamed x9, local copies, waits for them, and re-layouts  5.35 us

profile of v3, /device:TPU:8, one launch (start us, length us, event | category | flops | bytes accessed | tf_op | source)
XLA Modules:
  0.0 185.9 jit_solution(14235253227002904958)
XLA Ops:
  0.6 104.9 %train.1 = (bf16[512,1024]{1,0:T(8,128)(2,1)}, f32[512,1024]{1,0:T(8,128)}, bf16[1024,1024]{1,0:T(8,128)(2,1)}, bf16[1024,2816]{1,0:T(8,128)(2,1)}, bf16[1024,28...) custom-call(bf16[512,1024]{1,0:T(8,128)(2,1)} %tokens.1, ...), custom_call_target="tpu_custom_call" | custom-call | tf_op jit(solution)/shard_map/train/pallas_call | solution.py:700
  105.6 0.0 copy-start.2
  105.6 0.0 copy-start.1
  105.6 74.9 %reduce_products.1 = f32[1,1056896]{1,0:T(1,128)} custom-call(bf16[1024,1024]{1,0:T(8,128)(2,1)} %get-tuple-element.13.refs_0_, bf16[1024,2816]{1,0:T(8,128)(2,1)} %get-tuple-element.14.refs_1_, bf16[1024,2816]{1,0:T(8,128)(2,1)} %get-tuple-element.15.refs_2_, bf16[1024,2816]{1,0:T(8,128)(2,1)} %get-tuple-element.16.refs_3_, ...), custom_call_target="tpu_custom_call" | custom-call | tf_op jit(solution)/shard_map/reduce_products/pallas_call | solution.py:1318
  180.5 0.0 copy-done.2
  180.5 0.0 copy-start
  180.5 1.0 copy.10
  181.5 0.0 copy-done.1
  181.5 1.3 copy.11
  182.8 1.0 copy-done
  183.9 2.0 %copy.12 = f32[1,1056896]{1,0:T(1,128)} copy(f32[1,1056896]{1,0:T(1,128)S(1)} %copy-done) | data formatting | bytes 8455168
Async XLA Ops:
  105.6 74.9 %copy-start.2 = (bf16[512,1024]{1,0:T(8,128)(2,1)S(1)}, bf16[512,1024]{1,0:T(8,128)(2,1)}, u32[]{:S(2)}) copy-start(bf16[512,1024]{1,0:T(8,128)(2,1)} %get-tuple-element.11) | copy-start | bytes 3145732
  105.6 75.9 %copy-start.1 = (f32[512,1024]{1,0:T(8,128)S(1)}, f32[512,1024]{1,0:T(8,128)}, u32[]{:S(2)}) copy-start(f32[512,1024]{1,0:T(8,128)} %get-tuple-element.12) | copy-start | bytes 6291460
  180.5 3.3 %copy-start = (f32[1,1056896]{1,0:T(1,128)S(1)}, f32[1,1056896]{1,0:T(1,128)}, u32[]{:S(2)}) copy-start(f32[1,1056896]{1,0:T(1,128)} %reduce_products.1) | copy-start | bytes 12682756

commit v4 on v3

--- a/solution.py
+++ b/solution.py
@@ -162,6 +162,7 @@
 
 ROWS = 128
 CHUNKS_OF = LEN // ROWS
+HANDS = 2
 
 
 def lanes_of_head(kind, block, half):
@@ -291,30 +292,34 @@
     def rows_at(step, phase=0):
         return pl.ds(pl.multiple_of(phase * count + step * ROWS, ROWS), ROWS)
 
-    def hand_on(step):
-        rows = rows_at(step)
+    def piece_at(step, piece, phase=0):
+        size = ROWS // HANDS
+        return pl.ds(pl.multiple_of(phase * count + step * ROWS + piece * size, size), size)
+
+    def hand_on(step, piece):
+        rows = piece_at(step, piece)
         return pltpu.make_async_remote_copy(
             src_ref=x_v.at[rows, :],
             dst_ref=z_v.at[rows, :],
-            send_sem=on_send.at[step],
-            recv_sem=on_recv.at[step],
+            send_sem=on_send.at[step, piece],
+            recv_sem=on_recv.at[step, piece],
             device_id=(section + 1, batch),
             device_id_type=MESH,
         )
 
-    def hand_back(step):
-        rows = rows_at(step)
+    def hand_back(step, piece):
+        rows = piece_at(step, piece)
         return pltpu.make_async_remote_copy(
             src_ref=x_v.at[rows, :],
             dst_ref=g_v.at[rows, :],
-            send_sem=back_send.at[step],
-            recv_sem=back_recv.at[step],
+            send_sem=back_send.at[step, piece],
+            recv_sem=back_recv.at[step, piece],
             device_id=(section - 1, batch),
             device_id_type=MESH,
         )
 
-    def far_copy(kind, step=0):
-        rows, target = rows_at(step), rows_at(step, 1)
+    def far_copy(kind, step=0, piece=0):
+        rows, target = piece_at(step, piece), piece_at(step, piece, 1)
         source, target = (
             (z_v.at[rows, :], z_v.at[target, :]),
             (g_v.at[rows, :], g_v.at[target, :]),
@@ -324,8 +329,8 @@
         return pltpu.make_async_remote_copy(
             src_ref=source,
             dst_ref=target,
-            send_sem=far_send.at[kind, step],
-            recv_sem=far_recv.at[kind, step],
+            send_sem=far_send.at[kind, step, piece],
+            recv_sem=far_recv.at[kind, step, piece],
             device_id=(section, far),
             device_id_type=MESH,
         )
@@ -337,7 +342,8 @@
     @pl.when(gives & (section == last))
     def _():
         for step in range(steps):
-            far_copy(1, step).start()
+            for piece in range(HANDS):
+                far_copy(1, step, piece).start()
 
     def act_out(step):
         rows = rows_at(step)
@@ -367,17 +373,19 @@
         rows, here = rows_at(step), rows_at(step, phase)
         own = phase == 0
 
-        @pl.when(own & (section > 0))
-        def _():
-            hand_on(step).wait_recv()
-
-        @pl.when(own & gives)
-        def _():
-            far_copy(0, step).start()
-
-        @pl.when(jnp.logical_not(own))
-        def _():
-            far_copy(0, step).wait_recv()
+        for piece in range(HANDS):
+
+            @pl.when(own & (section > 0))
+            def _(piece=piece):
+                hand_on(step, piece).wait_recv()
+
+            @pl.when(own & gives)
+            def _(piece=piece):
+                far_copy(0, step, piece).start()
+
+            @pl.when(jnp.logical_not(own))
+            def _(piece=piece):
+                far_copy(0, step, piece).wait_recv()
 
         z = z_v[here, :].astype(F32)
         scaled = lax.rsqrt(jnp.mean(z * z, axis=1, keepdims=True) + EPSILON)
@@ -390,7 +398,8 @@
 
             @pl.when(section < last)
             def _():
-                hand_on(step).start()
+                for piece in range(HANDS):
+                    hand_on(step, piece).start()
 
             act_out(step).start()
 
@@ -401,17 +410,19 @@
         rows, here = rows_at(step), rows_at(step, phase)
         own = phase == 0
 
-        @pl.when(own & (section < last))
-        def _():
-            hand_back(step).wait_recv()
-
-            @pl.when(gives)
-            def _():
-                far_copy(1, step).start()
-
-        @pl.when(jnp.logical_not(own))
-        def _():
-            far_copy(1, step).wait_recv()
+        for piece in range(HANDS):
+
+            @pl.when(own & (section < last))
+            def _(piece=piece):
+                hand_back(step, piece).wait_recv()
+
+                @pl.when(gives)
+                def _():
+                    far_copy(1, step, piece).start()
+
+            @pl.when(jnp.logical_not(own))
+            def _(piece=piece):
+                far_copy(1, step, piece).wait_recv()
 
         unhidden(here, rows)
 
@@ -421,7 +432,8 @@
 
             @pl.when(section < last)
             def _():
-                hand_on(step).wait_send()
+                for piece in range(HANDS):
+                    hand_on(step, piece).wait_send()
 
             act_out(step).wait()
             z = z_v[rows, :].astype(F32)
@@ -437,7 +449,8 @@
 
             @pl.when(section > 0)
             def _():
-                hand_back(step).start()
+                for piece in range(HANDS):
+                    hand_back(step, piece).start()
 
             gradient_out(step).start()
 
@@ -657,7 +670,8 @@
             def _():
                 @pl.when(section > 0)
                 def _():
-                    hand_back(step).wait_send()
+                    for piece in range(HANDS):
+                        hand_back(step, piece).wait_send()
 
                 gradient_out(step).wait()
 
@@ -685,7 +699,8 @@
     def _():
         for kind in range(2):
             for step in range(steps):
-                far_copy(kind, step).wait_send()
+                for piece in range(HANDS):
+                    far_copy(kind, step, piece).wait_send()
         far_copy(2).wait_send()
         far_copy(3).wait_send()
 
@@ -743,12 +758,12 @@
             pltpu.SemaphoreType.DMA((2,)),
             pltpu.SemaphoreType.DMA((3, steps)),
             pltpu.SemaphoreType.DMA((4, steps)),
-            pltpu.SemaphoreType.DMA((steps,)),
-            pltpu.SemaphoreType.DMA((steps,)),
-            pltpu.SemaphoreType.DMA((steps,)),
-            pltpu.SemaphoreType.DMA((steps,)),
-            pltpu.SemaphoreType.DMA((4, steps)),
-            pltpu.SemaphoreType.DMA((4, steps)),
+            pltpu.SemaphoreType.DMA((steps, HANDS)),
+            pltpu.SemaphoreType.DMA((steps, HANDS)),
+            pltpu.SemaphoreType.DMA((steps, HANDS)),
+            pltpu.SemaphoreType.DMA((steps, HANDS)),
+            pltpu.SemaphoreType.DMA((4, steps, HANDS)),
+            pltpu.SemaphoreType.DMA((4, steps, HANDS)),
         ],
         compiler_params=pltpu.CompilerParams(
             collective_id=0, has_side_effects=True, vmem_limit_bytes=62 * MIB

time: 188 us -> 187 us (level)
  no operation moved by 1% of the time
where the time goes in v4:
time: 187 us
  Pallas kernels  181 us (97%)
  local copies, waits for them, and re-layouts  5.35 us (3%)
    pallas_call x1, Pallas kernels, train(): pl.pallas_call(functools.partial(train_kernel, swapping), out_shape=(jax....  106 us
    pallas_call x1, Pallas kernels, reduce_products(): pl.pallas_call(reduce_kernel, out_shape=jax.ShapeDtypeStruct((1, (step_ro...  74.9 us
    unnamed x9, local copies, waits for them, and re-layouts  5.35 us

profile of v4, /device:TPU:8, one launch (start us, length us, event | category | flops | bytes accessed | tf_op | source)
XLA Modules:
  0.0 186.5 jit_solution(15414197777775613615)
XLA Ops:
  0.6 105.6 %train.1 = (bf16[512,1024]{1,0:T(8,128)(2,1)}, f32[512,1024]{1,0:T(8,128)}, bf16[1024,1024]{1,0:T(8,128)(2,1)}, bf16[1024,2816]{1,0:T(8,128)(2,1)}, bf16[1024,28...) custom-call(bf16[512,1024]{1,0:T(8,128)(2,1)} %tokens.1, ...), custom_call_target="tpu_custom_call" | custom-call | tf_op jit(solution)/shard_map/train/pallas_call | solution.py:715
  106.3 0.0 copy-start.2
  106.3 0.0 copy-start.1
  106.3 74.9 %reduce_products.1 = f32[1,1056896]{1,0:T(1,128)} custom-call(bf16[1024,1024]{1,0:T(8,128)(2,1)} %get-tuple-element.13.refs_0_, bf16[1024,2816]{1,0:T(8,128)(2,1)} %get-tuple-element.14.refs_1_, bf16[1024,2816]{1,0:T(8,128)(2,1)} %get-tuple-element.15.refs_2_, bf16[1024,2816]{1,0:T(8,128)(2,1)} %get-tuple-element.16.refs_3_, ...), custom_call_target="tpu_custom_call" | custom-call | tf_op jit(solution)/shard_map/reduce_products/pallas_call | solution.py:1333
  181.2 0.0 copy-done.2
  181.2 0.0 copy-start
  181.2 1.0 copy.10
  182.2 0.0 copy-done.1
  182.2 1.3 copy.11
  183.5 1.0 copy-done
  184.5 2.0 %copy.12 = f32[1,1056896]{1,0:T(1,128)} copy(f32[1,1056896]{1,0:T(1,128)S(1)} %copy-done) | data formatting | bytes 8455168
Async XLA Ops:
  106.3 74.9 %copy-start.2 = (bf16[512,1024]{1,0:T(8,128)(2,1)S(1)}, bf16[512,1024]{1,0:T(8,128)(2,1)}, u32[]{:S(2)}) copy-start(bf16[512,1024]{1,0:T(8,128)(2,1)} %get-tuple-element.11) | copy-start | bytes 3145732
  106.3 75.9 %copy-start.1 = (f32[512,1024]{1,0:T(8,128)S(1)}, f32[512,1024]{1,0:T(8,128)}, u32[]{:S(2)}) copy-start(f32[512,1024]{1,0:T(8,128)} %get-tuple-element.12) | copy-start | bytes 6291460
  181.2 3.3 %copy-start = (f32[1,1056896]{1,0:T(1,128)S(1)}, f32[1,1056896]{1,0:T(1,128)}, u32[]{:S(2)}) copy-start(f32[1,1056896]{1,0:T(1,128)} %reduce_products.1) | copy-start | bytes 12682756

commit v5 on v4

--- a/solution.py
+++ b/solution.py
@@ -885,10 +885,10 @@
 
     def value_tile(self, out, k):
         some = pl.ds(0, MICRO * LEN)
-        left = self.left_v[k // 2, some, pl.ds(pl.multiple_of(lax.rem(k, 2) * 512, 512), 512)]
-        right = self.d_v[1, some, pl.ds(pl.multiple_of(k // 2 * D, D), D)]
-        scale = jnp.where(k < 2, SCALE, out_scale(LINEAR))
-        self.tall(out, left, right, 8, 512, HEAD_ROWS + 4096 * (k + 1), scale, 512)
+        left = self.left_v[k // 4, some, block256(lax.rem(k, 4))]
+        right = self.d_v[1, some, pl.ds(pl.multiple_of(k // 4 * D, D), D)]
+        scale = jnp.where(k < 4, SCALE, out_scale(LINEAR))
+        self.tall(out, left, right, 8, 256, HEAD_ROWS + 2048 * (k + 2), scale, 512)
 
 
 DOWN_ROW = HEAD_ROWS + 2 * PAIR_TILES * PAIR_ROWS
@@ -945,7 +945,7 @@
                 each(0, 16, lambda k: work.window_tile(out_v, k))
             else:
                 each(0, 2, lambda k: work.low_tile(out_v, k))
-                each(0, 4, lambda k: work.value_tile(out_v, k))
+                each(0, 8, lambda k: work.value_tile(out_v, k))
             done = WINDOW_END if kind == WINDOW else LINEAR_END
             clear(out_v, done, total - done)
 
@@ -1224,8 +1224,8 @@
 
         def value(k):
             work.value_tile(part, k)
-            start = HEAD_ROWS + 4096 * (k + 1)
-            stop = jnp.where(k == 3, cover, start + 4096)
+            start = HEAD_ROWS + 2048 * (k + 2)
+            stop = jnp.where(k == 7, cover, start + 2048)
             release(0, start, stop, limits[0])
             release(1, start - 2 * step_rows, stop - 2 * step_rows, limits[1])
 
@@ -1240,11 +1240,12 @@
 
         def value_and_on(k):
             value(k)
-            each(jnp.minimum(jnp.maximum(k - 1, 0), ahead), jnp.minimum(k, ahead), functools.partial(pass_on, 0))
+            done, next_done = jnp.maximum(k - 2, 0) // 2, jnp.maximum(k - 1, 0) // 2
+            each(jnp.minimum(done, ahead), jnp.minimum(next_done, ahead), functools.partial(pass_on, 0))
 
         each(0, 2, low)
         late(lambda copy: copy.wait())
-        each(0, 4, value_and_on)
+        each(0, 8, value_and_on)
 
         def own_count(to):
             return jnp.where(core == 0, limits[to][0], limits[to][1])

time: 187 us -> 186 us (level)
  no operation moved by 1% of the time
where the time goes in v5:
time: 186 us
  Pallas kernels  180 us (97%)
  local copies, waits for them, and re-layouts  5.35 us (3%)
    pallas_call x1, Pallas kernels, train(): pl.pallas_call(functools.partial(train_kernel, swapping), out_shape=(jax....  106 us
    pallas_call x1, Pallas kernels, reduce_products(): pl.pallas_call(reduce_kernel, out_shape=jax.ShapeDtypeStruct((1, (step_ro...  74.3 us
    unnamed x9, local copies, waits for them, and re-layouts  5.35 us

profile of v5, /device:TPU:8, one launch (start us, length us, event | category | flops | bytes accessed | tf_op | source)
XLA Modules:
  0.0 185.9 jit_solution(12955627870305372878)
XLA Ops:
  0.6 105.6 %train.1 = (bf16[512,1024]{1,0:T(8,128)(2,1)}, f32[512,1024]{1,0:T(8,128)}, bf16[1024,1024]{1,0:T(8,128)(2,1)}, bf16[1024,2816]{1,0:T(8,128)(2,1)}, bf16[1024,28...) custom-call(bf16[512,1024]{1,0:T(8,128)(2,1)} %tokens.1, ...), custom_call_target="tpu_custom_call" | custom-call | tf_op jit(solution)/shard_map/train/pallas_call | solution.py:715
  106.3 0.0 copy-start.2
  106.3 0.0 copy-start.1
  106.3 74.3 %reduce_products.1 = f32[1,1056896]{1,0:T(1,128)} custom-call(bf16[1024,1024]{1,0:T(8,128)(2,1)} %get-tuple-element.13.refs_0_, bf16[1024,2816]{1,0:T(8,128)(2,1)} %get-tuple-element.14.refs_1_, bf16[1024,2816]{1,0:T(8,128)(2,1)} %get-tuple-element.15.refs_2_, bf16[1024,2816]{1,0:T(8,128)(2,1)} %get-tuple-element.16.refs_3_, ...), custom_call_target="tpu_custom_call" | custom-call | tf_op jit(solution)/shard_map/reduce_products/pallas_call | solution.py:1334
  180.6 0.0 copy-done.2
  180.6 0.0 copy-start
  180.6 1.0 copy.10
  181.5 0.0 copy-done.1
  181.6 1.3 copy.11
  182.9 1.0 copy-done
  183.9 2.0 %copy.12 = f32[1,1056896]{1,0:T(1,128)} copy(f32[1,1056896]{1,0:T(1,128)S(1)} %copy-done) | data formatting | bytes 8455168
Async XLA Ops:
  106.3 74.3 %copy-start.2 = (bf16[512,1024]{1,0:T(8,128)(2,1)S(1)}, bf16[512,1024]{1,0:T(8,128)(2,1)}, u32[]{:S(2)}) copy-start(bf16[512,1024]{1,0:T(8,128)(2,1)} %get-tuple-element.11) | copy-start | bytes 3145732
  106.3 75.3 %copy-start.1 = (f32[512,1024]{1,0:T(8,128)S(1)}, f32[512,1024]{1,0:T(8,128)}, u32[]{:S(2)}) copy-start(f32[512,1024]{1,0:T(8,128)} %get-tuple-element.12) | copy-start | bytes 6291460
  180.6 3.3 %copy-start = (f32[1,1056896]{1,0:T(1,128)S(1)}, f32[1,1056896]{1,0:T(1,128)}, u32[]{:S(2)}) copy-start(f32[1,1056896]{1,0:T(1,128)} %reduce_products.1) | copy-start | bytes 12682756
